TPU v7x, 128 devices: a whole 4x4x4 slice. The times are simulated.
128 devices in a mesh: seq: 16 (over z, y_lo, core), chan: 8 (over y_hi, x).
Axes of the slice: x: 4, y: 4 (y_hi: 2, y_lo: 2; y = y_hi * 2 + y_lo), z: 4, core: 2. Of those that a mesh axis runs over, the one named last changes fastest.
Arguments:
- inputs: bfloat16 [16384, 4096], P('seq', 'chan'), may hold values from -6 to 6
- out_grad: bfloat16 [16384, 4096], P('seq', 'chan'), may hold values from -6 to 6
- out_weight: bfloat16 [4096, 4096], P('chan'), may hold values from -0.09375 to 0.09375
- filt: float32 [2048, 4096], P('seq', 'chan'), may hold values from -1.2 to 1.2
Outputs:
- grad_in: bfloat16 [16384, 4096], P('seq', 'chan')
- filt_grad: float32 [2048, 4096], P('seq', 'chan')
All inputs are finite; a program needn't handle non-finite values.
Results may differ from a plain program's by a relative error of at most 0.0049.
Values may be sent and summed in bfloat16 or wider, within the bound.
A program may use at most 256 MiB of HBM per device.

v0:
```python
import math

import jax
import jax.numpy as jnp
from jax import lax
from jax.sharding import PartitionSpec as P

LAG_STEPS = 2
BLOCK = 256


highest = lax.Precision.HIGHEST
higher = lax.Precision.HIGH


def from_behind(block, axis, distance):
    devices = range(lax.axis_size(axis))
    route = [(i - distance, i) for i in devices if i - distance in devices]
    return lax.ppermute(block, axis, route)


def per_device(inputs, out_grad, out_weight, filt):
    span_len, chan_width = inputs.shape
    block_len = BLOCK
    frame_len = 2 * BLOCK
    mixed_sum = lax.dot_general(
        lax.all_gather(out_grad, "chan", axis=1, tiled=True),
        out_weight,
        (((1,), (1,)), ((), ())),
        preferred_element_type=jnp.float32,
    )
    grad_mix = mixed_sum.astype(jnp.bfloat16)
    whole_filter = lax.all_gather(filt, "seq", axis=0, tiled=True)
    later_list = [from_behind(grad_mix, "seq", -offset) for offset in range(1, LAG_STEPS + 1)]
    extended = jnp.concatenate([grad_mix] + later_list, axis=0)
    freq_index = lax.iota(jnp.int32, frame_len)[:, None]
    time_index = lax.iota(jnp.int32, block_len)[None, :]
    angles = (freq_index * time_index % frame_len).astype(jnp.float32) * (2.0 * math.pi / frame_len)
    cos_table = jnp.cos(angles)
    sin_table = jnp.sin(angles)
    parity = jnp.where(lax.iota(jnp.int32, frame_len) % 2 == 0, 1.0, -1.0).astype(jnp.float32)[
        None, :, None
    ]

    def spectrum(blocks, level):
        real_part = jnp.einsum("fb,nbc->nfc", cos_table, blocks, precision=level)
        imag_part = -jnp.einsum("fb,nbc->nfc", sin_table, blocks, precision=level)
        return (real_part, imag_part)

    def inverse(real_part, imag_part):
        front = jnp.einsum("fa,nfc->nac", cos_table, real_part, precision=highest)
        back = jnp.einsum("fa,nfc->nac", sin_table, imag_part, precision=highest)
        return (front - back) / frame_len

    base_real, base_imag = spectrum(
        extended.astype(jnp.float32).reshape(-1, block_len, chan_width), higher
    )
    win_real = base_real[:-1] + parity * base_real[1:]
    win_imag = base_imag[:-1] + parity * base_imag[1:]
    lag_real, lag_imag = spectrum(whole_filter.reshape(-1, block_len, chan_width), highest)
    val_real, val_imag = spectrum(
        inputs.astype(jnp.float32).reshape(-1, block_len, chan_width), higher
    )
    lag_count = lag_real.shape[0]
    block_count = val_real.shape[0]

    def add_lag(lag_index, totals):
        slice_real = lax.dynamic_slice_in_dim(win_real, lag_index, block_count, 0)
        slice_imag = lax.dynamic_slice_in_dim(win_imag, lag_index, block_count, 0)
        coef_real = lax.dynamic_index_in_dim(lag_real, lag_index, 0, keepdims=False)
        coef_imag = lax.dynamic_index_in_dim(lag_imag, lag_index, 0, keepdims=False)
        return (
            totals[0] + coef_real * slice_real + coef_imag * slice_imag,
            totals[1] + coef_real * slice_imag - coef_imag * slice_real,
        )

    empty_in = jnp.zeros((block_count, frame_len, chan_width), jnp.float32)
    sum_real, sum_imag = lax.fori_loop(0, lag_count, add_lag, (empty_in, empty_in))

    def add_block(block_index, totals):
        slice_real = lax.dynamic_slice_in_dim(win_real, block_index, lag_count, 0)
        slice_imag = lax.dynamic_slice_in_dim(win_imag, block_index, lag_count, 0)
        coef_real = lax.dynamic_index_in_dim(val_real, block_index, 0, keepdims=False)
        coef_imag = lax.dynamic_index_in_dim(val_imag, block_index, 0, keepdims=False)
        return (
            totals[0] + coef_real * slice_real + coef_imag * slice_imag,
            totals[1] + coef_real * slice_imag - coef_imag * slice_real,
        )

    empty_lag = jnp.zeros((lag_count, frame_len, chan_width), jnp.float32)
    grad_real, grad_imag = lax.fori_loop(0, block_count, add_block, (empty_lag, empty_lag))
    grad_in = inverse(sum_real, sum_imag).reshape(span_len, chan_width).astype(jnp.bfloat16)
    local_grad = inverse(grad_real, grad_imag).reshape(-1, chan_width)
    seq_count = lax.axis_size("seq")
    grad_scale = 1.0 / math.sqrt(span_len * seq_count)
    owned = lax.psum_scatter(local_grad, "seq", scatter_dimension=0, tiled=True)
    filt_grad = owned * grad_scale
    return (grad_in, filt_grad)


def solution(mesh):
    in_specs = (P("seq", "chan"), P("seq", "chan"), P("chan", None), P("seq", "chan"))
    out_specs = (P("seq", "chan"), P("seq", "chan"))
    return jax.shard_map(
        per_device, mesh=mesh, in_specs=in_specs, out_specs=out_specs, check_vma=False
    )
```

profile of v0, /device:TPU:1, one launch (start us, length us, event | category | flops | bytes accessed | tf_op | source)
XLA Modules:
  0.0 508.7 jit_solution(2675074448289331453)
XLA Ops:
  8.7 124.4 %all-gather.5.cloned.1.call-done = bf16[1024,4096]{1,0:T(8,128)(2,1)} async-done(((bf16[1024,512]{1,0:T(8,128)(2,1)}), bf16[1024,4096]{1,0:T(8,128)(2,1)}) %all-gather.5.cloned.1.call-update) | async-done | bytes 8388624 | tf_op jit(solution)/shard_map/all_gather | solution.py:27
  133.1 9.1 %convolution_convert_fusion = bf16[1024,512]{1,0:T(8,128)(2,1)S(1)} fusion(bf16[1024,4096]{1,0:T(8,128)(2,1)} %all-gather.5.cloned.1.call-done, bf16[512,4096]{1,0:T(8,128)(2,1)} %param.10), kind=kOutput, calls=%fused_computation.25 | convolution fusion | flops 4295491584 | bytes 13631488 | tf_op jit(solution)/shard_map/dot_general | solution.py:26
  156.6 47.9 %all-gather.3.cloned.1.call-done = f32[2048,512]{1,0:T(8,128)} async-done(((f32[128,512]{1,0:T(8,128)}), f32[2048,512]{1,0:T(8,128)}) %all-gather.3.cloned.1.call-update) | async-done | bytes 4194320 | tf_op jit(solution)/shard_map/all_gather | solution.py:33
  204.5 14.5 %convolution_bitcast_fusion.1 = f32[8,512,512]{2,1,0:T(8,128)} fusion(f32[8,256,512]{2,1,0:T(8,128)} %bitcast.77), kind=kOutput, calls=%fused_computation.21 | convolution fusion | flops 6444285952 | bytes 12582912 | tf_op jit(solution)/shard_map/fb,nbc->nfc/dot_general | solution.py:46
  226.3 9.9 %negate_bitcast_fusion = f32[12,512,512]{1,2,0:T(8,128)} fusion(bf16[12,256,512]{2,1,0:T(8,128)(2,1)S(1)} %bitcast.76), kind=kOutput, calls=%fused_computation.12 | convolution fusion | flops 4836818944 | bytes 15728640 | tf_op jit(solution)/shard_map/fb,nbc->nfc/dot_general | solution.py:47
  236.2 16.4 %fusion.4 = (f32[11,512,512]{1,2,0:T(8,128)}, f32[11,512,512]{1,2,0:T(8,128)}) fusion(f32[12,512,512]{1,2,0:T(8,128)} %negate_bitcast_fusion, f32[512]{0:T(512)S(1)} %fusion.39, f32[12,512,512]{1,2,0:T(8,128)S(1)} %convolution_bitcast_fusion), kind=kLoop, calls=%fused_computation.14 | loop fusion | flops 11534336 | bytes 69208064 | tf_op jit(solution)/shard_map/add | solution.py:59
  252.5 12.1 %copy.12 = f32[11,512,512]{2,1,0:T(8,128)} copy(f32[11,512,512]{1,2,0:T(8,128)} %get-tuple-element.355) | data formatting | bytes 23068672
  264.7 12.1 %copy.13 = f32[11,512,512]{2,1,0:T(8,128)} copy(f32[11,512,512]{1,2,0:T(8,128)} %get-tuple-element.354) | data formatting | bytes 23068672
  276.8 77.0 %while.33 = (s32[]{:T(128)}, f32[8,512,512]{2,1,0:T(8,128)}, f32[8,512,512]{2,1,0:T(8,128)}, f32[4,512,512]{2,1,0:T(8,128)}, f32[11,512,512]{2,1,0:T(8,128)}, /*...) while((s32[]{:T(128)}, f32[8,512,512]{2,1,0:T(8,128)}, ...), condition=%wide.region_3.4_spmd.clone, body=%wide.region_2.3_spmd.clone.sunk | while | flops 20971524 | bytes 56623212 | solution.py:91
  278.9 11.9 %fusion.96 = (f32[8,512,512]{2,1,0:T(8,128)}, f32[8,512,512]{2,1,0:T(8,128)}) fusion(f32[8,512,512]{2,1,0:T(8,128)} %get-tuple-element.496, f32[11,512,512]{2,1,0:T(8,128)} %get-tuple-element.509, s32[]{:T(128)} %get-tuple-element.494, f32[11,512,512]{2,1,0:T(8,128)} %get-tuple-element.507, f32[512,512]{1,0:T(8,128)S(1)} %get-tuple-element.454, ...), kind=kLoop, calls=%fused_computation.7.clone.1 | loop fusion | flops 20971520 | bytes 52428804 | tf_op jit(solution)/shard_map/while/body/eval_jaxpr/sub | solution.py:87
  292.6 19.3 %fusion.96 = (f32[8,512,512]{2,1,0:T(8,128)}, f32[8,512,512]{2,1,0:T(8,128)}) fusion(f32[8,512,512]{2,1,0:T(8,128)} %get-tuple-element.496, f32[11,512,512]{2,1,0:T(8,128)} %get-tuple-element.509, s32[]{:T(128)} %get-tuple-element.494, f32[11,512,512]{2,1,0:T(8,128)} %get-tuple-element.507, f32[512,512]{1,0:T(8,128)S(1)} %get-tuple-element.454, ...), kind=kLoop, calls=%fused_computation.7.clone.1 | loop fusion | flops 20971520 | bytes 52428804 | tf_op jit(solution)/shard_map/while/body/eval_jaxpr/sub | solution.py:87
  313.6 19.3 %fusion.96 = (f32[8,512,512]{2,1,0:T(8,128)}, f32[8,512,512]{2,1,0:T(8,128)}) fusion(f32[8,512,512]{2,1,0:T(8,128)} %get-tuple-element.496, f32[11,512,512]{2,1,0:T(8,128)} %get-tuple-element.509, s32[]{:T(128)} %get-tuple-element.494, f32[11,512,512]{2,1,0:T(8,128)} %get-tuple-element.507, f32[512,512]{1,0:T(8,128)S(1)} %get-tuple-element.454, ...), kind=kLoop, calls=%fused_computation.7.clone.1 | loop fusion | flops 20971520 | bytes 52428804 | tf_op jit(solution)/shard_map/while/body/eval_jaxpr/sub | solution.py:87
  334.6 19.3 %fusion.96 = (f32[8,512,512]{2,1,0:T(8,128)}, f32[8,512,512]{2,1,0:T(8,128)}) fusion(f32[8,512,512]{2,1,0:T(8,128)} %get-tuple-element.496, f32[11,512,512]{2,1,0:T(8,128)} %get-tuple-element.509, s32[]{:T(128)} %get-tuple-element.494, f32[11,512,512]{2,1,0:T(8,128)} %get-tuple-element.507, f32[512,512]{1,0:T(8,128)S(1)} %get-tuple-element.454, ...), kind=kLoop, calls=%fused_computation.7.clone.1 | loop fusion | flops 20971520 | bytes 52428804 | tf_op jit(solution)/shard_map/while/body/eval_jaxpr/sub | solution.py:87
  353.8 14.5 %fusion.15 = f32[8,512,256]{1,2,0:T(8,128)S(1)} fusion(f32[8,512,512]{2,1,0:T(8,128)} %get-tuple-element.254), kind=kOutput, calls=%fused_computation.38 | convolution fusion | flops 6444285952 | bytes 12582912 | tf_op jit(solution)/shard_map/fa,nfc->nac/dot_general | solution.py:51
  368.4 13.7 %subtract_multiply_fusion = f32[8,512,256]{1,2,0:T(8,128)} fusion(f32[8,512,256]{1,2,0:T(8,128)S(1)} %fusion.15, f32[8,512,512]{2,1,0:T(8,128)S(1)} %copy-done.2), kind=kOutput, calls=%fused_computation.19 | convolution fusion | flops 6446383104 | bytes 16777216 | tf_op jit(solution)/shard_map/fa,nfc->nac/dot_general | solution.py:52
  382.2 14.6 %negate_bitcast_fusion.1 = f32[8,512,512]{2,1,0:T(8,128)} fusion(f32[8,256,512]{2,1,0:T(8,128)} %bitcast.78), kind=kOutput, calls=%fused_computation.17 | convolution fusion | flops 6446383104 | bytes 12582912 | tf_op jit(solution)/shard_map/fb,nbc->nfc/dot_general | solution.py:47
  396.8 88.3 %while.32 = (s32[]{:T(128)}, f32[4,512,512]{2,1,0:T(8,128)}, f32[4,512,512]{2,1,0:T(8,128)}, f32[8,512,512]{2,1,0:T(8,128)}, f32[11,512,512]{2,1,0:T(8,128)}, /*...) while((s32[]{:T(128)}, f32[4,512,512]{2,1,0:T(8,128)}, ...), condition=%wide.region_1.2_spmd.clone, body=%wide.region_0.1_spmd.clone.sunk | while | flops 10485763 | bytes 31457388 | solution.py:78
  407.1 9.9 %fusion.95 = (f32[4,512,512]{2,1,0:T(8,128)}, f32[4,512,512]{2,1,0:T(8,128)}) fusion(f32[4,512,512]{2,1,0:T(8,128)} %get-tuple-element.469, f32[11,512,512]{2,1,0:T(8,128)} %get-tuple-element.482, s32[]{:T(128)} %get-tuple-element.467, f32[11,512,512]{2,1,0:T(8,128)} %get-tuple-element.480, f32[512,512]{1,0:T(8,128)S(1)} %get-tuple-element.443, ...), kind=kLoop, calls=%fused_computation.1.clone.1 | loop fusion | flops 10485760 | bytes 27262980 | tf_op jit(solution)/shard_map/while/body/eval_jaxpr/sub | solution.py:74
  418.7 9.7 %fusion.95 = (f32[4,512,512]{2,1,0:T(8,128)}, f32[4,512,512]{2,1,0:T(8,128)}) fusion(f32[4,512,512]{2,1,0:T(8,128)} %get-tuple-element.469, f32[11,512,512]{2,1,0:T(8,128)} %get-tuple-element.482, s32[]{:T(128)} %get-tuple-element.467, f32[11,512,512]{2,1,0:T(8,128)} %get-tuple-element.480, f32[512,512]{1,0:T(8,128)S(1)} %get-tuple-element.443, ...), kind=kLoop, calls=%fused_computation.1.clone.1 | loop fusion | flops 10485760 | bytes 27262980 | tf_op jit(solution)/shard_map/while/body/eval_jaxpr/sub | solution.py:74
  430.2 9.8 %fusion.95 = (f32[4,512,512]{2,1,0:T(8,128)}, f32[4,512,512]{2,1,0:T(8,128)}) fusion(f32[4,512,512]{2,1,0:T(8,128)} %get-tuple-element.469, f32[11,512,512]{2,1,0:T(8,128)} %get-tuple-element.482, s32[]{:T(128)} %get-tuple-element.467, f32[11,512,512]{2,1,0:T(8,128)} %get-tuple-element.480, f32[512,512]{1,0:T(8,128)S(1)} %get-tuple-element.443, ...), kind=kLoop, calls=%fused_computation.1.clone.1 | loop fusion | flops 10485760 | bytes 27262980 | tf_op jit(solution)/shard_map/while/body/eval_jaxpr/sub | solution.py:74
  441.6 9.7 %fusion.95 = (f32[4,512,512]{2,1,0:T(8,128)}, f32[4,512,512]{2,1,0:T(8,128)}) fusion(f32[4,512,512]{2,1,0:T(8,128)} %get-tuple-element.469, f32[11,512,512]{2,1,0:T(8,128)} %get-tuple-element.482, s32[]{:T(128)} %get-tuple-element.467, f32[11,512,512]{2,1,0:T(8,128)} %get-tuple-element.480, f32[512,512]{1,0:T(8,128)S(1)} %get-tuple-element.443, ...), kind=kLoop, calls=%fused_computation.1.clone.1 | loop fusion | flops 10485760 | bytes 27262980 | tf_op jit(solution)/shard_map/while/body/eval_jaxpr/sub | solution.py:74
  453.1 9.4 %fusion.95 = (f32[4,512,512]{2,1,0:T(8,128)}, f32[4,512,512]{2,1,0:T(8,128)}) fusion(f32[4,512,512]{2,1,0:T(8,128)} %get-tuple-element.469, f32[11,512,512]{2,1,0:T(8,128)} %get-tuple-element.482, s32[]{:T(128)} %get-tuple-element.467, f32[11,512,512]{2,1,0:T(8,128)} %get-tuple-element.480, f32[512,512]{1,0:T(8,128)S(1)} %get-tuple-element.443, ...), kind=kLoop, calls=%fused_computation.1.clone.1 | loop fusion | flops 10485760 | bytes 27262980 | tf_op jit(solution)/shard_map/while/body/eval_jaxpr/sub | solution.py:74
  464.2 9.4 %fusion.95 = (f32[4,512,512]{2,1,0:T(8,128)}, f32[4,512,512]{2,1,0:T(8,128)}) fusion(f32[4,512,512]{2,1,0:T(8,128)} %get-tuple-element.469, f32[11,512,512]{2,1,0:T(8,128)} %get-tuple-element.482, s32[]{:T(128)} %get-tuple-element.467, f32[11,512,512]{2,1,0:T(8,128)} %get-tuple-element.480, f32[512,512]{1,0:T(8,128)S(1)} %get-tuple-element.443, ...), kind=kLoop, calls=%fused_computation.1.clone.1 | loop fusion | flops 10485760 | bytes 27262980 | tf_op jit(solution)/shard_map/while/body/eval_jaxpr/sub | solution.py:74
  475.4 9.4 %fusion.95 = (f32[4,512,512]{2,1,0:T(8,128)}, f32[4,512,512]{2,1,0:T(8,128)}) fusion(f32[4,512,512]{2,1,0:T(8,128)} %get-tuple-element.469, f32[11,512,512]{2,1,0:T(8,128)} %get-tuple-element.482, s32[]{:T(128)} %get-tuple-element.467, f32[11,512,512]{2,1,0:T(8,128)} %get-tuple-element.480, f32[512,512]{1,0:T(8,128)S(1)} %get-tuple-element.443, ...), kind=kLoop, calls=%fused_computation.1.clone.1 | loop fusion | flops 10485760 | bytes 27262980 | tf_op jit(solution)/shard_map/while/body/eval_jaxpr/sub | solution.py:74
  (44 shorter events, 67.6 us)
Async XLA Ops:
  7.2 140.0 %copy-start = (bf16[1024,512]{1,0:T(8,128)(2,1)S(1)}, bf16[1024,512]{1,0:T(8,128)(2,1)}, u32[]{:S(2)}) copy-start(bf16[1024,512]{1,0:T(8,128)(2,1)} %param.8) | copy-start | bytes 3145732
  7.2 125.9 %all-gather.5.cloned.1.call-start = ((), (), s32[]{:S(2)}) async-start(), calls=%async_computation.2 | async-start | bytes 9437184 | tf_op jit(solution)/shard_map/all_gather | solution.py:27
  7.9 196.6 %all-gather.3.cloned.1.call-start = ((), (), s32[]{:S(2)}) async-start(), calls=%async_computation.1 | async-start | bytes 4456448 | tf_op jit(solution)/shard_map/all_gather | solution.py:33
  8.7 491.6 %reduce-scatter.2.cloned.1.call-start = ((), (), s32[]{:S(2)}) async-start(), calls=%async_computation.3 | async-start | bytes 4456448 | tf_op jit(solution)/shard_map/reduce_scatter | solution.py:96
  142.2 76.8 %collective-permute-start = (bf16[1024,512]{1,0:T(8,128)(2,1)S(1)}, bf16[1024,512]{1,0:T(8,128)(2,1)S(1)}, u32[]{:S(2)}, u32[]{:S(2)}) collective-permute-start(bf16[1024,512]{1,0:T(8,128)(2,1)S(1)} %convolution_convert_fusion), channel_id=1, source_target_pairs={{8,0},{16,8},{24,16},{32,24},{40,32},{48,40},{56,48},{64,56},{72,6... | collective-permute-start | bytes 3145736 | tf_op jit(solution)/shard_map/ppermute | solution.py:19
  145.7 73.4 %collective-permute-start.1 = (bf16[1024,512]{1,0:T(8,128)(2,1)S(1)}, bf16[1024,512]{1,0:T(8,128)(2,1)}, u32[]{:S(2)}, u32[]{:S(2)}) collective-permute-start(bf16[1024,512]{1,0:T(8,128)(2,1)S(1)} %convolution_convert_fusion), channel_id=1, source_target_pairs={{16,0},{24,8},{32,16},{40,24},{48,32},{56,40},{64,48},{72,56},{80,... | collective-permute-start | bytes 3145736 | tf_op jit(solution)/shard_map/ppermute | solution.py:19
  353.8 14.6 %copy-start.2 = (f32[8,512,512]{2,1,0:T(8,128)S(1)}, f32[8,512,512]{2,1,0:T(8,128)}, u32[]{:S(2)}) copy-start(f32[8,512,512]{2,1,0:T(8,128)} %get-tuple-element.255) | copy-start | bytes 25165828
  485.0 8.2 %copy-start.3 = (f32[4,512,512]{2,1,0:T(8,128)S(1)}, f32[4,512,512]{2,1,0:T(8,128)}, u32[]{:S(2)}) copy-start(f32[4,512,512]{2,1,0:T(8,128)} %get-tuple-element.253) | copy-start | bytes 12582916
  485.0 16.9 %copy-start.1 = (bf16[1024,512]{1,0:T(8,128)(2,1)S(1)}, bf16[1024,512]{1,0:T(8,128)(2,1)}, u32[]{:S(2)}) copy-start(bf16[1024,512]{1,0:T(8,128)(2,1)} %param.8) | copy-start | bytes 3145732
Sparse Core Ops, SparseCore 0:
  10.2 122.8 all-gather.4
  134.8 69.6 all-gather.2
  382.3 69.3 reduce-scatter.1
where the time goes:
time: 515 us; the launch traced here: 509 us
  waiting for transfers between devices  174 us (34%)
  other arithmetic  164 us (32%)
  matrix products  107 us (21%)
  local copies, waits for them, and re-layouts  44.9 us (9%)
  between operations  14.1 us (3%)
    all_gather x1, waiting for transfers between devices, per_device(): lax.all_gather(out_grad, 'chan', axis=1, tiled=True)  124 us
    sub x8, other arithmetic, add_lag(): totals[1] + coef_real * slice_imag - coef_imag * slice_real  74.2 us
    sub x4, other arithmetic, add_block(): totals[1] + coef_real * slice_imag - coef_imag * slice_real  69.7 us
    all_gather x1, waiting for transfers between devices, per_device(): whole_filter = lax.all_gather(filt, 'seq', axis=0, tiled=True)  47.9 us
    dot_general x3, matrix products, spectrum(): imag_part = -jnp.einsum('fb,nbc->nfc', sin_table, blocks, precision=level)  29.2 us
    dot_general x3, matrix products, spectrum(): real_part = jnp.einsum('fb,nbc->nfc', cos_table, blocks, precision=level)  24.9 us
    unnamed x10, local copies, waits for them, and re-layouts  24.3 us
    dot_general x2, matrix products, inverse(): front = jnp.einsum('fa,nfc->nac', cos_table, real_part, precision=highest)  22.7 us
  transfers between devices with their start and end apart: 5, of which 2 were waited for; matrix products, arithmetic and copies ran while one was open for 30% of the time, Pallas kernels for 0%

commit v1 on v0

v1 whole, which is shorter than its diff:
```python
import math

import jax
import jax.numpy as jnp
import numpy as np
from jax import lax
from jax.experimental import pallas as pl
from jax.experimental.pallas import tpu as pltpu
from jax.sharding import PartitionSpec as P

BLOCK = 256
FRAME = 2 * BLOCK
HALF = FRAME // 2
ROWS = 8
LANES = 128


def split_table(table):
    high = table.astype(jnp.bfloat16)
    low = (table - high.astype(np.float32)).astype(jnp.bfloat16)
    return high, low


def tables(scale):
    freq = np.arange(HALF, dtype=np.int64)[:, None]
    time = np.arange(FRAME, dtype=np.int64)[None, :]
    angle = ((2 * freq + 1) * time % (2 * FRAME)).astype(np.float64) * (math.pi / FRAME)
    forward = np.concatenate([np.cos(angle), -np.sin(angle)], axis=0)
    backward = forward[:, :BLOCK].T * (2.0 / FRAME)
    result = []
    for table in (forward, backward):
        result.extend(split_table(table.astype(np.float32)))
    return result


def dot(a, b):
    return lax.dot_general(a, b, (((1,), (0,)), ((), ())), preferred_element_type=jnp.float32)


def conv_kernel(
    grad_ref, in_ref, filt_ref, fwd_hi, fwd_lo, bwd_hi, bwd_lo,
    out_ref, lag_ref, win, lag, val, acc_in, acc_lag,
):
    blocks, lags = val.shape[0], lag.shape[0]
    width = in_ref.shape[1]

    @pl.loop(0, lags)
    def _(m):
        part = filt_ref[pl.ds(pl.multiple_of(m * BLOCK, BLOCK), BLOCK), :]
        lag[m] = dot(fwd_hi[:, :BLOCK], part) + dot(fwd_lo[:, :BLOCK], part)

    @pl.loop(0, blocks)
    def _(n):
        part = in_ref[pl.ds(pl.multiple_of(n * BLOCK, BLOCK), BLOCK), :]
        val[n] = dot(fwd_hi[:, :BLOCK], part) + dot(fwd_lo[:, :BLOCK], part)

    @pl.loop(0, blocks + lags - 1)
    def _(i):
        part = grad_ref[pl.ds(pl.multiple_of(i * BLOCK, BLOCK), FRAME), :]
        win[i] = dot(fwd_hi[...], part) + dot(fwd_lo[...], part)

    @pl.loop(0, HALF // ROWS)
    def _(p):
        re = pl.ds(pl.multiple_of(p * ROWS, ROWS), ROWS)
        im = pl.ds(pl.multiple_of(HALF + p * ROWS, ROWS), ROWS)

        @pl.loop(0, width // LANES)
        def _(q):
            ch = pl.ds(pl.multiple_of(q * LANES, LANES), LANES)
            f = [(lag[m, re, ch], lag[m, im, ch]) for m in range(lags)]
            v = [(val[n, re, ch], val[n, im, ch]) for n in range(blocks)]
            a = [None] * blocks
            d = [None] * lags

            def add(total, k, w):
                r = k[0] * w[0] + k[1] * w[1]
                s = k[0] * w[1] - k[1] * w[0]
                return (r, s) if total is None else (total[0] + r, total[1] + s)

            for i in range(blocks + lags - 1):
                w = (win[i, re, ch], win[i, im, ch])
                for n in range(blocks):
                    m = i - n
                    if 0 <= m < lags:
                        a[n] = add(a[n], f[m], w)
                        d[m] = add(d[m], v[n], w)
            for n in range(blocks):
                acc_in[n, re, ch], acc_in[n, im, ch] = a[n]
            for m in range(lags):
                acc_lag[m, re, ch], acc_lag[m, im, ch] = d[m]

    @pl.loop(0, blocks)
    def _(n):
        part = acc_in[n].astype(jnp.bfloat16)
        rows = pl.ds(pl.multiple_of(n * BLOCK, BLOCK), BLOCK)
        out_ref[rows, :] = (dot(bwd_hi[...], part) + dot(bwd_lo[...], part)).astype(out_ref.dtype)

    @pl.loop(0, lags)
    def _(m):
        part = acc_lag[m].astype(jnp.bfloat16)
        rows = pl.ds(pl.multiple_of(m * BLOCK, BLOCK), BLOCK)
        lag_ref[rows, :] = (dot(bwd_hi[...], part) + dot(bwd_lo[...], part)).astype(lag_ref.dtype)


def convolve(extended, inputs, filt):
    span, width = inputs.shape
    lag_len = filt.shape[0]
    blocks, lags = span // BLOCK, lag_len // BLOCK
    vmem = pl.BlockSpec(memory_space=pltpu.VMEM)
    return pl.pallas_call(
        conv_kernel,
        out_shape=(
            jax.ShapeDtypeStruct((span, width), jnp.bfloat16),
            jax.ShapeDtypeStruct((lag_len, width), jnp.bfloat16),
        ),
        in_specs=[vmem] * 7,
        out_specs=(vmem, vmem),
        scratch_shapes=[
            pltpu.VMEM((blocks + lags - 1, FRAME, width), jnp.float32),
            pltpu.VMEM((lags, FRAME, width), jnp.float32),
            pltpu.VMEM((blocks, FRAME, width), jnp.float32),
            pltpu.VMEM((blocks, FRAME, width), jnp.float32),
            pltpu.VMEM((lags, FRAME, width), jnp.float32),
        ],
        compiler_params=pltpu.CompilerParams(vmem_limit_bytes=60 << 20),
        name="convolve",
    )(extended, inputs, filt, *tables(1.0))


def from_behind(block, axis, distance):
    devices = range(lax.axis_size(axis))
    route = [(i - distance, i) for i in devices if i - distance in devices]
    return lax.ppermute(block, axis, route)


def per_device(inputs, out_grad, out_weight, filt):
    span_len, chan_width = inputs.shape
    grad_mix = lax.dot_general(
        lax.all_gather(out_grad, "chan", axis=1, tiled=True),
        out_weight,
        (((1,), (1,)), ((), ())),
        preferred_element_type=jnp.float32,
    ).astype(jnp.bfloat16)
    whole_filter = lax.all_gather(filt.astype(jnp.bfloat16), "seq", axis=0, tiled=True)
    steps = whole_filter.shape[0] // span_len
    later = [from_behind(grad_mix, "seq", -offset) for offset in range(1, steps + 1)]
    extended = jnp.concatenate([grad_mix] + later, axis=0)
    grad_in, local_grad = convolve(extended, inputs, whole_filter)
    seq_count = lax.axis_size("seq")
    parts = lax.all_to_all(
        local_grad.reshape(seq_count, -1, chan_width), "seq", 0, 0, tiled=True
    )
    grad_scale = 1.0 / math.sqrt(span_len * seq_count)
    filt_grad = jnp.sum(parts.astype(jnp.float32), axis=0) * grad_scale
    return (grad_in, filt_grad)


def solution(mesh):
    in_specs = (P("seq", "chan"), P("seq", "chan"), P("chan", None), P("seq", "chan"))
    out_specs = (P("seq", "chan"), P("seq", "chan"))
    return jax.shard_map(
        per_device, mesh=mesh, in_specs=in_specs, out_specs=out_specs, check_vma=False
    )
```

time: 515 us -> 275 us (0.53); the launches traced: 509 us -> 275 us
  other arithmetic: 164 us -> 4.39 us
  matrix products: 107 us -> 9.09 us
  local copies, waits for them, and re-layouts: 44.9 us -> 0 us
  Pallas kernels: 0 us -> 33.1 us
  blocking collectives: 0 us -> 30.5 us
    sub x12 -> x0, other arithmetic: 144 us -> none  [the longest x8 74.2 us: add_lag(): totals[1] + coef_real * slice_imag - coef_imag * slice_real]
    dot_general x10 -> x0, matrix products: 97.7 us -> none  [the longest x3 29.2 us: spectrum(): imag_part = -jnp.einsum('fb,nbc->nfc', sin_table, blocks, precision=level)]
    ppermute x2, waiting for transfers between devices: 0.01 us -> 34.7 us  [from_behind(): return lax.ppermute(block, axis, route)]
    pallas_call x0 -> x1, Pallas kernels: none -> 33.1 us  [convolve(): pl.pallas_call(conv_kernel, out_shape=(jax.ShapeDtypeStruct((span, width)...]
    all_to_all x0 -> x1, blocking collectives: none -> 30.5 us  [per_device(): lax.all_to_all(local_grad.reshape(seq_count, -1, chan_width), 'seq', 0, 0...]
    all_gather x1, waiting for transfers between devices: 47.9 us -> 19.9 us  [per_device(): lax.all_gather(filt.astype(jnp.bfloat16), 'seq', axis=0, tiled=True)]
    unnamed x10 -> x0, local copies, waits for them, and re-layouts: 24.3 us -> none
    mul x12 -> x0, local copies, waits for them, and re-layouts: 20.6 us -> none  [the longest x8 13.8 us: add_lag(): coef_imag * slice_imag]
  transfers between devices with their start and end apart: 5 -> 4, of which waited for: 2 -> 4; matrix products, arithmetic and copies ran while one was open for 30% -> 5% of each run, Pallas kernels for 0% -> 0%
where the time goes in v1:
time: 275 us
  waiting for transfers between devices  179 us (65%)
  Pallas kernels  33.1 us (12%)
  blocking collectives  30.5 us (11%)
  between operations  14.1 us (5%)
  matrix products  9.09 us (3%)
  starting transfers between devices  4.82 us (2%)
  other arithmetic  4.39 us (2%)
    all_gather x1, waiting for transfers between devices, per_device(): lax.all_gather(out_grad, 'chan', axis=1, tiled=True)  123 us
    ppermute x2, waiting for transfers between devices, from_behind(): return lax.ppermute(block, axis, route)  34.7 us
    pallas_call x1, Pallas kernels, convolve(): pl.pallas_call(conv_kernel, out_shape=(jax.ShapeDtypeStruct((span, width)...  33.1 us
    all_to_all x1, blocking collectives, per_device(): lax.all_to_all(local_grad.reshape(seq_count, -1, chan_width), 'seq', 0, 0...  30.5 us
    all_gather x1, waiting for transfers between devices, per_device(): lax.all_gather(filt.astype(jnp.bfloat16), 'seq', axis=0, tiled=True)  19.9 us
    dot_general x1, matrix products, per_device(): lax.dot_general(lax.all_gather(out_grad, 'chan', axis=1, tiled=True), out...  9.09 us
  transfers between devices with their start and end apart: 4, of which 4 were waited for; matrix products, arithmetic and copies ran while one was open for 5% of the time, Pallas kernels for 0%

profile of v1, /device:TPU:1, one launch (start us, length us, event | category | flops | bytes accessed | tf_op | source)
XLA Modules:
  0.0 274.7 jit_solution(13919171109987017571)
XLA Ops:
  7.2 0.0 all-gather.3.cloned.1.call-start
  7.2 0.7 all-gather.3.cloned.1.call-update
  7.9 0.0 all-gather.5.cloned.1.call-start
  7.9 1.6 convert_element_type.10
  9.6 0.0 all-gather.5.cloned.1.call-update
  9.6 123.5 %all-gather.3.cloned.1.call-done = bf16[1024,4096]{1,0:T(8,128)(2,1)} async-done(((bf16[1024,512]{1,0:T(8,128)(2,1)}), bf16[1024,4096]{1,0:T(8,128)(2,1)}) %all-gather.3.cloned.1.call-update) | async-done | bytes 8388624 | tf_op jit(solution)/shard_map/all_gather | solution.py:139
  133.1 9.1 %convolution_convert_fusion = bf16[1024,512]{1,0:T(8,128)(2,1)S(1)} fusion(bf16[1024,4096]{1,0:T(8,128)(2,1)} %all-gather.3.cloned.1.call-done, bf16[512,4096]{1,0:T(8,128)(2,1)} %param.10), kind=kOutput, calls=%fused_computation.2 | convolution fusion | flops 4295491584 | bytes 13631488 | tf_op jit(solution)/shard_map/dot_general | solution.py:138
  142.2 1.3 collective-permute-start.1
  143.5 3.5 %collective-permute-start = (bf16[1024,512]{1,0:T(8,128)(2,1)S(1)}, bf16[1024,512]{1,0:T(8,128)(2,1)S(1)}, u32[]{:S(2)}, u32[]{:S(2)}) collective-permute-start(bf16[1024,512]{1,0:T(8,128)(2,1)S(1)} %convolution_convert_fusion), channel_id=1, source_target_pairs={{8,0},{16,8},{24,16},{32,24},{40,32},{48,40},{56,48},{64,56},{72,6... | collective-permute-start | bytes 3145736 | tf_op jit(solution)/shard_map/ppermute | solution.py:133
  146.9 22.7 %collective-permute-done.1 = bf16[1024,512]{1,0:T(8,128)(2,1)S(1)} collective-permute-done((bf16[1024,512]{1,0:T(8,128)(2,1)S(1)}, bf16[1024,512]{1,0:T(8,128)(2,1)S(1)}, u32[]{:S(2)}, u32[]{:S(2)}) %collective-permute-start.1) | collective-permute-done | bytes 1048608 | tf_op jit(solution)/shard_map/ppermute | solution.py:133
  169.7 11.9 %collective-permute-done = bf16[1024,512]{1,0:T(8,128)(2,1)S(1)} collective-permute-done((bf16[1024,512]{1,0:T(8,128)(2,1)S(1)}, bf16[1024,512]{1,0:T(8,128)(2,1)S(1)}, u32[]{:S(2)}, u32[]{:S(2)}) %collective-permute-start) | collective-permute-done | bytes 1048608 | tf_op jit(solution)/shard_map/ppermute | solution.py:133
  181.6 1.8 pad_maximum_fusion.grad_ref
  183.4 19.9 %all-gather.5.cloned.1.call-done.filt_ref = bf16[2048,512]{1,0:T(8,128)(2,1)} async-done(((bf16[128,512]{1,0:T(8,128)(2,1)}), bf16[2048,512]{1,0:T(8,128)(2,1)}) %all-gather.5.cloned.1.call-update) | async-done | bytes 2097168 | tf_op jit(solution)/shard_map/all_gather | solution.py:144
  203.3 33.1 %convolve.1 = (bf16[1024,512]{1,0:T(8,128)(2,1)}, bf16[2048,512]{1,0:T(8,128)(2,1)}) custom-call(bf16[3072,512]{1,0:T(8,128)(2,1)} %pad_maximum_fusion.grad_ref, bf16[1024,512]{1,0:T(8,128)(2,1)} %in_ref.1, bf16[2048,512]{1,0:T(8,128)(2,1)} %all-gather.5.cloned.1.call-done.filt_ref, bf16[512,512]{1,0:T(8,128)(2,1)} %constant.12.clone.fwd_hi, ...), custom_call_target="tpu_custom_call" | custom-call | tf_op jit(solution)/shard_map/convolve/pallas_call | solution.py:110
  236.4 30.5 %all_to_all.5 = bf16[16,128,512]{2,1,0:T(8,128)(2,1)S(1)} all-to-all(bf16[16,128,512]{2,1,0:T(8,128)(2,1)} %bitcast.3), channel_id=1, replica_groups=mesh['seq'=16,'chan'=8] {'seq'}, dimensions={0} | all-to-all | bytes 4194304 | tf_op jit(solution)/shard_map/all_to_all | solution.py:150
  266.9 0.3 convert_reduce_fusion
  267.2 0.7 broadcast_multiply_fusion
Async XLA Ops:
  7.2 125.9 %all-gather.3.cloned.1.call-start = ((), (), s32[]{:S(2)}) async-start(), calls=%async_computation.1 | async-start | bytes 9437184 | tf_op jit(solution)/shard_map/all_gather | solution.py:139
  7.9 195.4 %all-gather.5.cloned.1.call-start = ((), (), s32[]{:S(2)}) async-start(), calls=%async_computation.2 | async-start | bytes 2228224 | tf_op jit(solution)/shard_map/all_gather | solution.py:144
  142.2 27.5 %collective-permute-start.1 = (bf16[1024,512]{1,0:T(8,128)(2,1)S(1)}, bf16[1024,512]{1,0:T(8,128)(2,1)S(1)}, u32[]{:S(2)}, u32[]{:S(2)}) collective-permute-start(bf16[1024,512]{1,0:T(8,128)(2,1)S(1)} %convolution_convert_fusion), channel_id=1, source_target_pairs={{16,0},{24,8},{32,16},{40,24},{48,32},{56,40},{64,48},{72,56},{80,... | collective-permute-start | bytes 3145736 | tf_op jit(solution)/shard_map/ppermute | solution.py:133
  143.5 38.1 %collective-permute-start = (bf16[1024,512]{1,0:T(8,128)(2,1)S(1)}, bf16[1024,512]{1,0:T(8,128)(2,1)S(1)}, u32[]{:S(2)}, u32[]{:S(2)}) collective-permute-start(bf16[1024,512]{1,0:T(8,128)(2,1)S(1)} %convolution_convert_fusion), channel_id=1, source_target_pairs={{8,0},{16,8},{24,16},{32,24},{40,32},{48,40},{56,48},{64,56},{72,6... | collective-permute-start | bytes 3145736 | tf_op jit(solution)/shard_map/ppermute | solution.py:133
Sparse Core Ops, SparseCore 0:
  10.2 122.8 all-gather.2
  135.4 67.8 all-gather.4

commit v2 on v1

v2 whole, which is shorter than its diff:
```python
import functools
import math

import jax
import jax.numpy as jnp
import numpy as np
from jax import lax
from jax.experimental import pallas as pl
from jax.experimental.pallas import tpu as pltpu
from jax.sharding import PartitionSpec as P

MESH = pl.DeviceIdType.MESH
BLOCK = 256
FRAME = 2 * BLOCK
HALF = FRAME // 2
ROWS = 8
LANES = 128
SPANS = 16
GROUP = 4
RING = 4
SPAN = 1024
CHUNKS = SPAN // BLOCK
WIDTH = 512
LAG_LEN = 2048
LAG_ROWS = LAG_LEN // SPANS
LAGS = LAG_LEN // BLOCK
BLOCKS = GROUP * SPAN // BLOCK
WINDOWS = BLOCKS + LAGS - 1
SHARE = RING * WIDTH


def split_table(table):
    high = table.astype(jnp.bfloat16)
    low = (table - high.astype(np.float32)).astype(jnp.bfloat16)
    return high, low


def tables():
    freq = np.arange(HALF, dtype=np.int64)[:, None]
    time = np.arange(FRAME, dtype=np.int64)[None, :]
    angle = ((2 * freq + 1) * time % (2 * FRAME)).astype(np.float64) * (math.pi / FRAME)
    forward = np.concatenate([np.cos(angle), -np.sin(angle)], axis=0)
    backward = forward[:, :BLOCK].T * (2.0 / FRAME)
    result = []
    for table in (forward, backward):
        result.extend(split_table(table.astype(np.float32)))
    return result


def dot(a, b):
    return lax.dot_general(a, b, (((1,), (0,)), ((), ())), preferred_element_type=jnp.float32)


def dot_rows(a, b):
    return lax.dot_general(a, b, (((1,), (1,)), ((), ())), preferred_element_type=jnp.float32)


def at(start, size):
    return pl.ds(pl.multiple_of(start, size), size)


def kernel(
    in_ref, og_ref, w_ref, filt_ref, fwd_hi, fwd_lo, bwd_hi, bwd_lo,
    out_ref, fg_ref,
    side, other_w, filt_all, values, part, got, grad, win, lag, val, acc, acc_lag,
    lag_out, lag_got, out_buf,
    x_send, x_recv, w_send, w_recv, f_send, f_recv, v_send, v_recv,
    p_send, p_recv, h_send, h_recv, o_send, o_recv, r_send, r_recv, local_sem,
):
    s = lax.axis_index("seq")
    ch = lax.axis_index("chan")
    core = s % 2
    q = s % GROUP
    z = s // GROUP
    half = ch // RING
    x = ch % RING
    right = half * RING + (x + 1) % RING
    left = half * RING + (x + RING - 1) % RING
    mirror = (ch + RING) % (2 * RING)

    def device(seq, chan):
        return {"seq": seq, "chan": chan}

    def mate(k):
        return z * GROUP + (q + k) % GROUP

    def remote(src, dst, send, recv, seq, chan):
        return pltpu.make_async_remote_copy(
            src_ref=src, dst_ref=dst, send_sem=send, recv_sem=recv,
            device_id=device(seq, chan), device_id_type=MESH,
        )

    barrier = pltpu.get_barrier_semaphore()
    peers = [(s, right), (s, left)]
    peers += [(mate(k), mirror) for k in range(GROUP)]
    peers += [((s + k) % SPANS, ch) for k in range(1, SPANS)]
    for seq, chan in peers:
        pl.semaphore_signal(barrier, inc=1, device_id=device(seq, chan), device_id_type=MESH)
    pl.semaphore_wait(barrier, len(peers))

    def direct(t):
        rows = at(t * BLOCK, BLOCK)
        return [
            remote(og_ref.at[rows], side.at[d, rows], x_send.at[d, t], x_recv.at[d, t], s, to)
            for d, to in ((0, right), (1, left))
        ]

    def onward(t):
        first = at(t * BLOCK, BLOCK // 2)
        second = at(t * BLOCK + BLOCK // 2, BLOCK // 2)
        return [
            remote(side.at[0, first], side.at[2, first], x_send.at[2, t], x_recv.at[2, t], s, right),
            remote(side.at[1, second], side.at[2, second], x_send.at[3, t], x_recv.at[3, t], s, left),
        ]

    def weight(j):
        rows = at((core * 2 + j) * LANES, LANES)
        return remote(
            w_ref.at[rows, at((1 - half) * SHARE, SHARE)], other_w.at[rows],
            w_send.at[0, j], w_recv.at[0, j], mate(2), mirror,
        )

    def weight_mine(j):
        rows = at((core * 2 + j) * LANES, LANES)
        return remote(
            other_w.at[rows], other_w.at[rows],
            w_send.at[1, j], w_recv.at[1, j], s + 1 - 2 * core, ch,
        )

    def filter_to(k):
        to = (s + k) % SPANS
        return remote(
            filt_ref.at[:, at((to % GROUP) * LANES, LANES)], filt_all.at[at(s * LAG_ROWS, LAG_ROWS)],
            f_send.at[k], f_recv.at[k], to, ch,
        )

    def values_to(k):
        return remote(
            in_ref.at[:, at((q + k) % GROUP * LANES, LANES)], values.at[at(q * SPAN, SPAN)],
            v_send.at[k], v_recv.at[k], mate(k), ch,
        )

    def part_to(side_of, k, t):
        rows = at(t * BLOCK, BLOCK)
        return remote(
            part.at[side_of, (q + k) % GROUP, rows], got.at[side_of, q, rows],
            p_send.at[side_of, k, t], p_recv.at[side_of, k, t], mate(k), mirror if side_of else ch,
        )

    def halo(i, t):
        return remote(
            grad.at[at(i * SPAN + t * BLOCK, BLOCK)],
            grad.at[at((GROUP + i) * SPAN + t * BLOCK, BLOCK)],
            h_send.at[i, t], h_recv.at[i, t], (s + SPANS - GROUP) % SPANS, ch,
        )

    def out_to(k):
        return remote(
            out_buf.at[(q + k) % GROUP], out_ref.at[:, at(q * LANES, LANES)],
            o_send.at[k], o_recv.at[k], mate(k), ch,
        )

    def lag_to(k):
        to = (s + k) % SPANS
        return remote(
            lag_out.at[at(to * LAG_ROWS, LAG_ROWS)], lag_got.at[s],
            r_send.at[k], r_recv.at[k], to, ch,
        )

    def start(copies):
        for copy in copies:
            copy.start()

    start(direct(0))
    for j in range(2):
        weight(j).start()
    start(direct(1))
    for k in range(1, SPANS):
        filter_to(k).start()
    for k in range(1, GROUP):
        values_to(k).start()
    filter_own = pltpu.make_async_copy(
        filt_ref.at[:, at(q * LANES, LANES)], filt_all.at[at(s * LAG_ROWS, LAG_ROWS)], local_sem.at[0]
    )
    values_own = pltpu.make_async_copy(
        in_ref.at[:, at(q * LANES, LANES)], values.at[at(q * SPAN, SPAN)], local_sem.at[1]
    )
    filter_own.start()
    values_own.start()

    def pass_on(t):
        for copy in direct(t):
            copy.wait_recv()
        start(onward(t))
        if t + 2 < CHUNKS:
            start(direct(t + 2))

    def put(table, index, wide):
        table[2 * index] = wide[:, :LANES]
        table[2 * index + 1] = wide[:, LANES:]

    def transform_filter():
        filter_own.wait()
        for k in range(1, SPANS):
            filter_to(k).wait_recv()

        @pl.loop(0, LAGS // 2)
        def _(m):
            wide = jnp.concatenate(
                [filt_all[at((2 * m + e) * BLOCK, BLOCK), :] for e in range(2)], axis=1
            )
            high = wide.astype(jnp.bfloat16)
            low = (wide - high.astype(jnp.float32)).astype(jnp.bfloat16)
            put(lag, m, dot(fwd_hi[:, :BLOCK], high) + dot(fwd_lo[:, :BLOCK], high) + dot(fwd_hi[:, :BLOCK], low))

    def transform_values():
        values_own.wait()
        for k in range(1, GROUP):
            values_to(k).wait_recv()

        @pl.loop(0, BLOCKS // 2)
        def _(n):
            wide = jnp.concatenate(
                [values[at((2 * n + e) * BLOCK, BLOCK), :] for e in range(2)], axis=1
            )
            put(val, n, dot(fwd_hi[:, :BLOCK], wide) + dot(fwd_lo[:, :BLOCK], wide))

    def multiply(side_of, t):
        rows = at(t * BLOCK, BLOCK)
        total = None
        for d, block in enumerate((og_ref.at[rows], side.at[1, rows], side.at[2, rows], side.at[0, rows])):
            place = (x + d) % RING
            if side_of:
                cols = other_w[:, at(place * WIDTH, WIDTH)]
            else:
                cols = w_ref[:, at((half * RING + place) * WIDTH, WIDTH)]
            term = dot_rows(block[...], cols)
            total = term if total is None else total + term
        total = total.astype(jnp.bfloat16)
        for k in range(GROUP):
            part[side_of, k, rows] = total[:, k * LANES:(k + 1) * LANES]
        for k in range(GROUP):
            if side_of or k:
                part_to(side_of, k, t).start()

    def across(t):
        for copy in onward(t):
            copy.wait_recv()

    def add_up(t):
        rows = at(t * BLOCK, BLOCK)
        for k in range(GROUP):
            owner = (q + GROUP - k) % GROUP
            part_to(1, k, t).wait_recv()
            if k:
                part_to(0, k, t).wait_recv()
                near = got[0, owner, rows]
            else:
                near = part[0, owner, rows]
            total = near.astype(jnp.float32) + got[1, owner, rows].astype(jnp.float32)
            grad[at(owner * SPAN + t * BLOCK, BLOCK), :] = total.astype(jnp.bfloat16)
        for i in range(2):
            halo(i, t).start()

    pass_on(0)
    transform_filter()
    weight(0).wait_recv()
    weight_mine(0).start()
    pass_on(1)
    transform_values()
    across(0)
    multiply(0, 0)
    pass_on(2)
    across(1)
    multiply(0, 1)
    weight(1).wait_recv()
    weight_mine(1).start()
    for j in range(2):
        weight_mine(j).wait_recv()
    for t in range(2):
        multiply(1, t)
    pass_on(3)
    for t in range(2, CHUNKS):
        across(t)
        multiply(0, t)
        multiply(1, t)
    for t in range(CHUNKS):
        add_up(t)
    for t in range(CHUNKS):
        for i in range(2):
            halo(i, t).wait_recv()

    @pl.when(z == SPANS // GROUP - 1)
    def _():
        grad[GROUP * SPAN:, :] = jnp.zeros((2 * SPAN, LANES), jnp.bfloat16)

    @pl.loop(0, WINDOWS // 2)
    def _(i):
        wide = jnp.concatenate(
            [grad[pl.ds(pl.multiple_of((2 * i + e) * BLOCK, BLOCK), FRAME), :] for e in range(2)], axis=1
        )
        put(win, i, dot(fwd_hi[...], wide) + dot(fwd_lo[...], wide))

    last = grad[(WINDOWS - 1) * BLOCK:, :]
    win[WINDOWS - 1] = dot(fwd_hi[...], last) + dot(fwd_lo[...], last)

    def add(total, k, w):
        r = k[0] * w[0] + k[1] * w[1]
        i = k[0] * w[1] - k[1] * w[0]
        return (r, i) if total is None else (total[0] + r, total[1] + i)

    @pl.loop(0, HALF // ROWS)
    def _(p):
        re = at(p * ROWS, ROWS)
        im = at(HALF + p * ROWS, ROWS)
        f = [(lag[m, re, :], lag[m, im, :]) for m in range(LAGS)]
        sums = {}
        for i in range(WINDOWS):
            w = (win[i, re, :], win[i, im, :])
            for m in range(LAGS):
                n = i - m
                if 0 <= n < BLOCKS:
                    sums[n] = add(sums.get(n), f[m], w)
            done = i - LAGS + 1
            if done >= 0:
                acc[done, re, :], acc[done, im, :] = sums.pop(done)

    for k in (2, 3, 1, 0):
        place = (q + k) % GROUP
        for n in range(CHUNKS // 2):
            base = place * CHUNKS + 2 * n
            wide = jnp.concatenate([acc[base], acc[base + 1]], axis=1).astype(jnp.bfloat16)
            wide = (dot(bwd_hi[...], wide) + dot(bwd_lo[...], wide)).astype(jnp.bfloat16)
            for e in range(2):
                out_buf[place, (2 * n + e) * BLOCK:(2 * n + e + 1) * BLOCK, :] = wide[:, e * LANES:(e + 1) * LANES]
        if k:
            out_to(k).start()
    out_ref[:, at(q * LANES, LANES)] = out_buf[q]

    @pl.loop(0, HALF // ROWS)
    def _(p):
        re = at(p * ROWS, ROWS)
        im = at(HALF + p * ROWS, ROWS)
        sums = [None] * LAGS
        for i in range(WINDOWS):
            w = (win[i, re, :], win[i, im, :])
            for m in range(LAGS):
                n = i - m
                if 0 <= n < BLOCKS:
                    sums[m] = add(sums[m], (val[n, re, :], val[n, im, :]), w)
        for m in range(LAGS):
            acc_lag[m, re, :], acc_lag[m, im, :] = sums[m]

    for m in range(LAGS // 2):
        wide = jnp.concatenate([acc_lag[2 * m], acc_lag[2 * m + 1]], axis=1).astype(jnp.bfloat16)
        wide = (dot(bwd_hi[...], wide) + dot(bwd_lo[...], wide)).astype(jnp.bfloat16)
        for e in range(2):
            lag_out[(2 * m + e) * BLOCK:(2 * m + e + 1) * BLOCK, :] = wide[:, e * LANES:(e + 1) * LANES]
    for k in range(1, SPANS):
        lag_to(k).start()
    lag_got[s] = lag_out[at(s * LAG_ROWS, LAG_ROWS), :]

    for k in range(1, SPANS):
        lag_to(k).wait_recv()
    scale = 1.0 / math.sqrt(SPAN * SPANS)
    for c in range(GROUP):
        total = lag_got[c].astype(jnp.float32)
        for j in range(1, SPANS // GROUP):
            total = total + lag_got[j * GROUP + c].astype(jnp.float32)
        fg_ref[:, c * LANES:(c + 1) * LANES] = total * scale

    for t in range(CHUNKS):
        for copy in direct(t) + onward(t):
            copy.wait_send()
        for i in range(2):
            halo(i, t).wait_send()
        for k in range(GROUP):
            part_to(1, k, t).wait_send()
            if k:
                part_to(0, k, t).wait_send()
    for j in range(2):
        weight(j).wait_send()
        weight_mine(j).wait_send()
    for k in range(1, SPANS):
        filter_to(k).wait_send()
        lag_to(k).wait_send()
    for k in range(1, GROUP):
        values_to(k).wait_send()
        out_to(k).wait_send()
        out_to(k).wait_recv()


def per_device(inputs, out_grad, out_weight, filt):
    vmem = pl.BlockSpec(memory_space=pltpu.VMEM)
    bf16, f32 = jnp.bfloat16, jnp.float32
    pair = [(2, CHUNKS)] * 2
    counts = [(4, CHUNKS)] * 2 + [(2, 2)] * 2 + [(SPANS,)] * 2 + [(GROUP,)] * 2
    counts += [(2, GROUP, CHUNKS)] * 2 + pair + [(GROUP,)] * 2 + [(SPANS,)] * 2 + [(2,)]
    return pl.pallas_call(
        kernel,
        out_shape=(
            jax.ShapeDtypeStruct((SPAN, WIDTH), bf16),
            jax.ShapeDtypeStruct((LAG_ROWS, WIDTH), f32),
        ),
        in_specs=[vmem] * 8,
        out_specs=(vmem, vmem),
        scratch_shapes=[
            pltpu.VMEM((3, SPAN, WIDTH), bf16),
            pltpu.VMEM((WIDTH, SHARE), bf16),
            pltpu.VMEM((LAG_LEN, LANES), f32),
            pltpu.VMEM((GROUP * SPAN, LANES), bf16),
            pltpu.VMEM((2, GROUP, SPAN, LANES), bf16),
            pltpu.VMEM((2, GROUP, SPAN, LANES), bf16),
            pltpu.VMEM(((GROUP + 2) * SPAN, LANES), bf16),
            pltpu.VMEM((WINDOWS, FRAME, LANES), f32),
            pltpu.VMEM((LAGS, FRAME, LANES), f32),
            pltpu.VMEM((BLOCKS, FRAME, LANES), f32),
            pltpu.VMEM((BLOCKS, FRAME, LANES), f32),
            pltpu.VMEM((LAGS, FRAME, LANES), f32),
            pltpu.VMEM((LAG_LEN, LANES), bf16),
            pltpu.VMEM((SPANS, LAG_ROWS, LANES), bf16),
            pltpu.VMEM((GROUP, SPAN, LANES), bf16),
        ] + [pltpu.SemaphoreType.DMA(count) for count in counts],
        compiler_params=pltpu.CompilerParams(
            collective_id=0, has_side_effects=True, vmem_limit_bytes=60 << 20
        ),
        cost_estimate=pl.CostEstimate(
            flops=20_000_000_000, bytes_accessed=12 << 20, transcendentals=0
        ),
        name="hyena_back",
    )(inputs, out_grad, out_weight, filt, *tables())


def solution(mesh):
    in_specs = (P("seq", "chan"), P("seq", "chan"), P("chan", None), P("seq", "chan"))
    out_specs = (P("seq", "chan"), P("seq", "chan"))
    return jax.shard_map(
        per_device, mesh=mesh, in_specs=in_specs, out_specs=out_specs, check_vma=False
    )
```

time: 275 us -> 107 us (0.39)
  waiting for transfers between devices: 179 us -> 0 us
  Pallas kernels: 33.1 us -> 102 us
  blocking collectives: 30.5 us -> 0 us
  between operations: 14.1 us -> 0.64 us
  matrix products: 9.09 us -> 0 us
  starting transfers between devices: 4.82 us -> 0 us
  other arithmetic: 4.39 us -> 0 us
  local copies, waits for them, and re-layouts: 0 us -> 3.93 us
    all_gather x2 -> x0, waiting for transfers between devices: 143 us -> none  [the longest x1 123 us: per_device(): lax.all_gather(out_grad, 'chan', axis=1, tiled=True)]
    pallas_call x1, Pallas kernels: 33.1 us -> 102 us  [per_device(): pl.pallas_call(kernel, out_shape=(jax.ShapeDtypeStruct((SPAN, WIDTH), bf1...]
    ppermute x2 -> x0, waiting for transfers between devices: 34.7 us -> none  [from_behind(): return lax.ppermute(block, axis, route)]
    all_to_all x1 -> x0, blocking collectives: 30.5 us -> none  [per_device(): lax.all_to_all(local_grad.reshape(seq_count, -1, chan_width), 'seq', 0, 0...]
    dot_general x1 -> x0, matrix products: 9.09 us -> none  [per_device(): lax.dot_general(lax.all_gather(out_grad, 'chan', axis=1, tiled=True), out...]
    ppermute x2 -> x0, starting transfers between devices: 4.74 us -> none  [from_behind(): return lax.ppermute(block, axis, route)]
    unnamed x0 -> x2, local copies, waits for them, and re-layouts: none -> 3.93 us
  transfers between devices with their start and end apart: 4 -> 0, of which waited for: 4 -> 0; matrix products, arithmetic and copies ran while one was open for 5% -> 0% of each run, Pallas kernels for 0% -> 0%
where the time goes in v2:
time: 107 us; the launch traced here: 106 us
  Pallas kernels  102 us (95%)
  local copies, waits for them, and re-layouts  3.93 us (4%)
    pallas_call x1, Pallas kernels, per_device(): pl.pallas_call(kernel, out_shape=(jax.ShapeDtypeStruct((SPAN, WIDTH), bf1...  102 us
    unnamed x2, local copies, waits for them, and re-layouts  3.93 us

profile of v2, /device:TPU:1, one launch (start us, length us, event | category | flops | bytes accessed | tf_op | source)
XLA Modules:
  0.0 106.4 jit_solution(2751854450866851884)
XLA Ops:
  0.6 101.9 %hyena_back.1 = (bf16[1024,512]{1,0:T(8,128)(2,1)}, f32[128,512]{1,0:T(8,128)}) custom-call(bf16[1024,512]{1,0:T(8,128)(2,1)} %in_ref.1, bf16[1024,512]{1,0:T(8,128)(2,1)} %og_ref.1, bf16[512,4096]{1,0:T(8,128)(2,1)} %w_ref.1, f32[128,512]{1,0:T(8,128)} %filt_ref.1, bf16[512,512]{1,0:T(8,128)(2,1)} %constant.8.clone.fwd_hi, ...), custom_call_target="tpu_custom_call" | custom-call | flops 20000000000 | bytes 12582912 | tf_op jit(solution)/shard_map/hyena_back/pallas_call | solution.py:399
  102.5 2.3 %copy.12 = bf16[1024,512]{1,0:T(8,128)(2,1)} copy(bf16[1024,512]{1,0:T(8,128)(2,1)} %get-tuple-element.4) | data formatting | bytes 2097152
  104.8 1.7 %copy.13 = f32[128,512]{1,0:T(8,128)} copy(f32[128,512]{1,0:T(8,128)} %get-tuple-element.5) | data formatting | bytes 524288

commit v3 on v2

v3 whole, which is shorter than its diff:
```python
import math

import jax
import jax.numpy as jnp
import numpy as np
from jax import lax
from jax.experimental import pallas as pl
from jax.experimental.pallas import tpu as pltpu
from jax.sharding import PartitionSpec as P

MESH = pl.DeviceIdType.MESH
BLOCK = 256
FRAME = 2 * BLOCK
HALF = FRAME // 2
ROWS = 8
LANES = 128
SPANS = 16
GROUP = 4
RING = 4
SPAN = 1024
STEPS = ((0, 256), (256, 256), (512, 256), (768, 128), (896, 128))
PER_SPAN = SPAN // BLOCK
AHEAD = 2
WIDTH = 512
LAG_LEN = 2048
LAG_ROWS = LAG_LEN // SPANS
LAG_SHARE = GROUP * LAG_ROWS
LAGS = LAG_LEN // BLOCK
BLOCKS = GROUP * SPAN // BLOCK
WINDOWS = BLOCKS + LAGS - 1
SHARE = RING * WIDTH
PIECE = WIDTH // 2 // RING


def split_table(table):
    high = table.astype(jnp.bfloat16)
    low = (table - high.astype(np.float32)).astype(jnp.bfloat16)
    return high, low


def tables():
    freq = np.arange(HALF, dtype=np.int64)[:, None]
    time = np.arange(FRAME, dtype=np.int64)[None, :]
    angle = ((2 * freq + 1) * time % (2 * FRAME)).astype(np.float64) * (math.pi / FRAME)
    forward = np.concatenate([np.cos(angle), -np.sin(angle)], axis=0)
    backward = forward[:, :BLOCK].T * (2.0 / FRAME)
    result = []
    for table in (forward, backward):
        result.extend(split_table(table.astype(np.float32)))
    return result


def dot(a, b):
    return lax.dot_general(a, b, (((1,), (0,)), ((), ())), preferred_element_type=jnp.float32)


def dot_rows(a, b):
    return lax.dot_general(a, b, (((1,), (1,)), ((), ())), preferred_element_type=jnp.float32)


def at(start, size):
    return pl.ds(pl.multiple_of(start, size), size)


def kernel(
    in_ref, og_ref, w_ref, filt_ref, fwd_hi, fwd_lo, bwd_hi, bwd_lo,
    out_ref, fg_ref,
    own, own_w,
    side, other_w, filt_all, values, part, got, grad, win, lag, val, acc, acc_lag,
    lag_out, lag_got, lag_sum, out_buf,
    x_send, x_recv, w_send, w_recv, f_send, f_recv, v_send, v_recv,
    p_send, p_recv, h_send, h_recv, o_send, o_recv, r_send, r_recv, local_sem,
):
    s = lax.axis_index("seq")
    ch = lax.axis_index("chan")
    core = s % 2
    q = s % GROUP
    z = s // GROUP
    half = ch // RING
    x = ch % RING
    right = half * RING + (x + 1) % RING
    left = half * RING + (x + RING - 1) % RING
    mirror = (ch + RING) % (2 * RING)
    sibling = s + 1 - 2 * core
    sends = []

    def mate(k):
        return z * GROUP + (q + k) % GROUP

    def along(k):
        return (s + k * GROUP) % SPANS

    def remote(src, dst, send, recv, seq, chan):
        return pltpu.make_async_remote_copy(
            src_ref=src, dst_ref=dst, send_sem=send, recv_sem=recv,
            device_id={"seq": seq, "chan": chan}, device_id_type=MESH,
        )

    def start(*copies):
        for copy in copies:
            copy.start()
            sends.append(copy)

    filter_own = pltpu.make_async_copy(
        filt_ref.at[:, at(q * LANES, LANES)], filt_all.at[at(s * LAG_ROWS, LAG_ROWS)], local_sem.at[0]
    )
    own_load = pltpu.make_async_copy(og_ref, own, local_sem.at[1])
    weight_load = pltpu.make_async_copy(w_ref.at[:, at(half * SHARE, SHARE)], own_w, local_sem.at[2])
    values_own = pltpu.make_async_copy(
        in_ref.at[:, at(q * LANES, LANES)], values.at[at(q * SPAN, SPAN)], local_sem.at[3]
    )
    filter_own.start()
    own_load.start()
    weight_load.start()
    values_own.start()

    barrier = pltpu.get_barrier_semaphore()
    peers = [(s, right), (s, left)]
    peers += [(mate(k), mirror) for k in range(GROUP)]
    peers += [(mate(k), ch) for k in range(1, GROUP)]
    peers += [(along(k), ch) for k in range(1, RING)]
    for seq, chan in peers:
        pl.semaphore_signal(
            barrier, inc=1, device_id={"seq": seq, "chan": chan}, device_id_type=MESH
        )
    pl.semaphore_wait(barrier, len(peers))

    def step_rows(t):
        return pl.ds(*STEPS[t])

    def direct(t):
        rows = step_rows(t)
        return [
            remote(og_ref.at[rows], side.at[d, rows], x_send.at[d, t], x_recv.at[d, t], s, to)
            for d, to in ((0, right), (1, left))
        ]

    def onward(t):
        begin, size = STEPS[t]
        first = pl.ds(begin, size // 2)
        second = pl.ds(begin + size // 2, size // 2)
        return [
            remote(side.at[0, first], side.at[2, first], x_send.at[2, t], x_recv.at[2, t], s, right),
            remote(side.at[1, second], side.at[2, second], x_send.at[3, t], x_recv.at[3, t], s, left),
        ]

    def piece(k):
        return at(core * (WIDTH // 2) + (z + RING - k) % RING * PIECE, PIECE)

    def weight(k):
        return remote(
            w_ref.at[piece(k), at((1 - half) * SHARE, SHARE)], other_w.at[piece(k)],
            w_send.at[k], w_recv.at[k], mate(2), mirror,
        )

    def weight_along(k):
        return remote(
            other_w.at[piece(0)], other_w.at[piece(0)], w_send.at[k], w_recv.at[k], along(k), ch
        )

    def weight_over(k):
        return remote(
            other_w.at[piece(k)], other_w.at[piece(k)],
            w_send.at[RING + k], w_recv.at[RING + k], sibling, ch,
        )

    def filter_to(k):
        return remote(
            filt_ref.at[:, at((q + k) % GROUP * LANES, LANES)], filt_all.at[at(s * LAG_ROWS, LAG_ROWS)],
            f_send.at[0, k], f_recv.at[0, k], mate(k), ch,
        )

    def filter_along(k):
        rows = at(z * LAG_SHARE, LAG_SHARE)
        return remote(
            filt_all.at[rows], filt_all.at[rows], f_send.at[1, k], f_recv.at[1, k], along(k), ch
        )

    def values_to(k):
        return remote(
            in_ref.at[:, at((q + k) % GROUP * LANES, LANES)], values.at[at(q * SPAN, SPAN)],
            v_send.at[k], v_recv.at[k], mate(k), ch,
        )

    def part_to(side_of, k, t):
        rows = step_rows(t)
        return remote(
            part.at[side_of, (q + k) % GROUP, rows], got.at[side_of, q, rows],
            p_send.at[side_of, k, t], p_recv.at[side_of, k, t], mate(k), mirror if side_of else ch,
        )

    def halo(i, t):
        return remote(
            grad.at[pl.ds(i * SPAN + STEPS[t][0], STEPS[t][1])],
            grad.at[pl.ds((GROUP + i) * SPAN + STEPS[t][0], STEPS[t][1])],
            h_send.at[i, t], h_recv.at[i, t], along(RING - 1), ch,
        )

    def out_to(k):
        return remote(
            out_buf.at[(q + k) % GROUP], out_ref.at[:, at(q * LANES, LANES)],
            o_send.at[k], o_recv.at[k], mate(k), ch,
        )

    def lag_along(k):
        return remote(
            lag_out.at[at((z + k) % RING * LAG_SHARE, LAG_SHARE)], lag_got.at[z],
            r_send.at[0, k], r_recv.at[0, k], along(k), ch,
        )

    def lag_to(k):
        return remote(
            lag_sum.at[at((q + k) % GROUP * LAG_ROWS, LAG_ROWS)], fg_ref.at[:, at(q * LANES, LANES)],
            r_send.at[1, k], r_recv.at[1, k], mate(k), ch,
        )

    def pass_on(t):
        for copy in direct(t):
            copy.wait_recv()
        start(*onward(t))
        if t + AHEAD < len(STEPS):
            start(*direct(t + AHEAD))

    def put(table, first, second, wide):
        table[first] = wide[:, :LANES]
        table[second] = wide[:, LANES:]

    def forward(wide):
        width = wide.shape[0]
        return dot(fwd_hi[:, :width], wide) + dot(fwd_lo[:, :width], wide)

    def backward(wide):
        wide = wide.astype(jnp.bfloat16)
        return (dot(bwd_hi[...], wide) + dot(bwd_lo[...], wide)).astype(jnp.bfloat16)

    def transform_filter():
        for k in range(1, RING):
            filter_along(k).wait_recv()

        @pl.loop(0, LAGS // 2)
        def _(m):
            wide = jnp.concatenate(
                [filt_all[at((2 * m + e) * BLOCK, BLOCK), :] for e in range(2)], axis=1
            )
            high = wide.astype(jnp.bfloat16)
            low = (wide - high.astype(jnp.float32)).astype(jnp.bfloat16)
            put(lag, 2 * m, 2 * m + 1, forward(high) + dot(fwd_hi[:, :BLOCK], low))

    def transform_values():
        values_own.wait()
        for k in range(1, GROUP):
            values_to(k).wait_recv()

        @pl.loop(0, BLOCKS // 2)
        def _(n):
            put(val, 2 * n, 2 * n + 1, forward(jnp.concatenate(
                [values[at((2 * n + e) * BLOCK, BLOCK), :] for e in range(2)], axis=1
            )))

    def window(i):
        return grad[pl.ds(pl.multiple_of(i * BLOCK, BLOCK), FRAME), :]

    def transform_windows(first, pairs):
        @pl.loop(0, pairs)
        def _(j):
            i = first + 2 * PER_SPAN * j
            put(win, i, i + PER_SPAN, forward(jnp.concatenate([window(i), window(i + PER_SPAN)], axis=1)))

    def multiply(side_of, t):
        rows = step_rows(t)
        weights = other_w if side_of else own_w
        total = None
        for d, block in enumerate((own.at[rows], side.at[1, rows], side.at[2, rows], side.at[0, rows])):
            term = dot_rows(block[...], weights[:, at((x + d) % RING * WIDTH, WIDTH)])
            total = term if total is None else total + term
        total = total.astype(jnp.bfloat16)
        for k in range(GROUP):
            part[side_of, k, rows] = total[:, k * LANES:(k + 1) * LANES]
        for k in (2, 3, 1, 0):
            if side_of or k:
                start(part_to(side_of, k, t))

    def across(t):
        for copy in onward(t):
            copy.wait_recv()

    def add_up(t):
        rows = step_rows(t)
        for k in range(GROUP):
            owner = (q + GROUP - k) % GROUP
            part_to(1, k, t).wait_recv()
            if k:
                part_to(0, k, t).wait_recv()
                near = got[0, owner, rows]
            else:
                near = part[0, owner, rows]
            total = near.astype(jnp.float32) + got[1, owner, rows].astype(jnp.float32)
            begin, size = STEPS[t]
            grad[pl.ds(pl.multiple_of(owner * SPAN + begin, LANES), size), :] = total.astype(jnp.bfloat16)
        for i in range(2):
            start(halo(i, t))

    def edge(t):
        for i in range(2):
            halo(i, t).wait_recv()

        @pl.when(z == RING - 1)
        def _():
            for i in range(2):
                begin, size = STEPS[t]
                grad[pl.ds((GROUP + i) * SPAN + begin, size), :] = jnp.zeros((size, LANES), jnp.bfloat16)

    def add(total, k, w):
        r = k[0] * w[0] + k[1] * w[1]
        i = k[0] * w[1] - k[1] * w[0]
        return (r, i) if total is None else (total[0] + r, total[1] + i)

    def bins(p):
        return at(p * ROWS, ROWS), at(HALF + p * ROWS, ROWS)

    def sum_inputs(place, classes, fresh):
        base = place * PER_SPAN

        @pl.loop(0, HALF // ROWS)
        def _(p):
            re, im = bins(p)
            f = [(lag[m, re, :], lag[m, im, :]) for m in range(LAGS)]
            sums = [None if fresh else (acc[base + n, re, :], acc[base + n, im, :]) for n in range(PER_SPAN)]
            for i in range(PER_SPAN + LAGS - 1):
                if i % PER_SPAN in classes:
                    w = (win[base + i, re, :], win[base + i, im, :])
                    for n in range(PER_SPAN):
                        if 0 <= i - n < LAGS:
                            sums[n] = add(sums[n], f[i - n], w)
            for n in range(PER_SPAN):
                acc[base + n, re, :], acc[base + n, im, :] = sums[n]

    def sum_lags(classes, fresh):
        @pl.loop(0, HALF // ROWS)
        def _(p):
            re, im = bins(p)
            sums = [None if fresh else (acc_lag[m, re, :], acc_lag[m, im, :]) for m in range(LAGS)]
            for i in range(WINDOWS):
                if i % PER_SPAN in classes:
                    w = (win[i, re, :], win[i, im, :])
                    for m in range(LAGS):
                        n = i - m
                        if 0 <= n < BLOCKS:
                            sums[m] = add(sums[m], (val[n, re, :], val[n, im, :]), w)
            for m in range(LAGS):
                acc_lag[m, re, :], acc_lag[m, im, :] = sums[m]

    start(*direct(0))
    start(weight(0), weight(2))
    for k in range(1, GROUP):
        start(filter_to(k))
    start(*direct(1))
    for k in range(1, GROUP):
        start(values_to(k))
    weight(0).wait_recv()
    start(weight_along(1), weight_along(3), weight_over(0))
    pass_on(0)
    weight(2).wait_recv()
    start(weight_over(2))
    for k in (1, 3):
        weight_along(k).wait_recv()
        start(weight_over(k))
    filter_own.wait()
    for k in range(1, GROUP):
        filter_to(k).wait_recv()
    start(*[filter_along(k) for k in (2, 1, 3)])
    pass_on(1)
    transform_values()
    own_load.wait()
    weight_load.wait()
    across(0)
    multiply(0, 0)
    for k in range(RING):
        weight_over(k).wait_recv()
    multiply(1, 0)
    pass_on(2)
    across(1)
    multiply(1, 1)
    multiply(0, 1)
    add_up(0)
    pass_on(3)
    transform_filter()
    across(2)
    multiply(1, 2)
    multiply(0, 2)
    pass_on(4)
    add_up(1)
    edge(0)
    edge(1)
    across(3)
    multiply(1, 3)
    multiply(0, 3)
    across(4)
    multiply(1, 4)
    multiply(0, 4)
    transform_windows(0, 3)
    for k in range(GROUP):
        sum_inputs((q + k) % GROUP, (0,), True)
    sum_lags((0,), True)
    add_up(2)
    edge(2)
    transform_windows(1, 3)
    add_up(3)
    add_up(4)
    for k in range(GROUP):
        sum_inputs((q + k) % GROUP, (1,), False)
    sum_lags((1,), False)
    edge(3)
    edge(4)
    transform_windows(PER_SPAN - 2, 3)
    transform_windows(PER_SPAN - 1, 2)
    final = (WINDOWS - 1) - (WINDOWS - 1 - (PER_SPAN - 1)) % PER_SPAN
    win[final] = forward(window(final))

    def finish_span(k):
        place = (q + k) % GROUP
        sum_inputs(place, (2, 3), False)
        for n in range(PER_SPAN // 2):
            base = place * PER_SPAN + 2 * n
            wide = backward(jnp.concatenate([acc[base], acc[base + 1]], axis=1))
            for e in range(2):
                out_buf[place, (2 * n + e) * BLOCK:(2 * n + e + 1) * BLOCK, :] = wide[:, e * LANES:(e + 1) * LANES]
        if k:
            start(out_to(k))

    finish_span(2)
    finish_span(3)
    sum_lags((2, 3), False)
    for k in (2, 1, 3, 0):
        place = (z + k) % RING
        wide = backward(jnp.concatenate([acc_lag[2 * place], acc_lag[2 * place + 1]], axis=1))
        for e in range(2):
            lag_out[at((2 * place + e) * BLOCK, BLOCK), :] = wide[:, e * LANES:(e + 1) * LANES]
        if k:
            start(lag_along(k))
    finish_span(1)
    finish_span(0)
    out_ref[:, at(q * LANES, LANES)] = out_buf[q]
    total = lag_out[at(z * LAG_SHARE, LAG_SHARE), :].astype(jnp.float32)
    for k in range(1, RING):
        lag_along(k).wait_recv()
        total = total + lag_got[(z + RING - k) % RING].astype(jnp.float32)
    lag_sum[...] = total * (1.0 / math.sqrt(SPAN * SPANS))
    for k in (2, 3, 1):
        start(lag_to(k))
    fg_ref[:, at(q * LANES, LANES)] = lag_sum[at(q * LAG_ROWS, LAG_ROWS), :]
    for copy in sends:
        copy.wait_send()
    for k in range(1, GROUP):
        out_to(k).wait_recv()
        lag_to(k).wait_recv()


def hand_over(out_ref, fg_ref, out_final, fg_final):
    out_final[...] = out_ref[...]
    fg_final[...] = fg_ref[...]


def per_device(inputs, out_grad, out_weight, filt):
    vmem = pl.BlockSpec(memory_space=pltpu.VMEM)
    anywhere = pl.BlockSpec(memory_space=pl.ANY)
    bf16, f32 = jnp.bfloat16, jnp.float32
    steps = len(STEPS)
    counts = [(4, steps)] * 2 + [(2 * RING,)] * 2 + [(2, GROUP)] * 2 + [(GROUP,)] * 2
    counts += [(2, GROUP, steps)] * 2 + [(2, steps)] * 2 + [(GROUP,)] * 2 + [(2, GROUP)] * 2 + [(4,)]
    results = pl.pallas_call(
        kernel,
        out_shape=(
            jax.ShapeDtypeStruct((SPAN, WIDTH), bf16),
            jax.ShapeDtypeStruct((LAG_ROWS, WIDTH), f32),
        ),
        in_specs=[anywhere] * 4 + [vmem] * 4,
        out_specs=(vmem, vmem),
        scratch_shapes=[
            pltpu.VMEM((SPAN, WIDTH), bf16),
            pltpu.VMEM((WIDTH, SHARE), bf16),
            pltpu.VMEM((3, SPAN, WIDTH), bf16),
            pltpu.VMEM((WIDTH, SHARE), bf16),
            pltpu.VMEM((LAG_LEN, LANES), f32),
            pltpu.VMEM((GROUP * SPAN, LANES), bf16),
            pltpu.VMEM((2, GROUP, SPAN, LANES), bf16),
            pltpu.VMEM((2, GROUP, SPAN, LANES), bf16),
            pltpu.VMEM(((GROUP + 2) * SPAN, LANES), bf16),
            pltpu.VMEM((WINDOWS, FRAME, LANES), f32),
            pltpu.VMEM((LAGS, FRAME, LANES), f32),
            pltpu.VMEM((BLOCKS, FRAME, LANES), f32),
            pltpu.VMEM((BLOCKS, FRAME, LANES), f32),
            pltpu.VMEM((LAGS, FRAME, LANES), f32),
            pltpu.VMEM((LAG_LEN, LANES), bf16),
            pltpu.VMEM((RING, LAG_SHARE, LANES), bf16),
            pltpu.VMEM((LAG_SHARE, LANES), f32),
            pltpu.VMEM((GROUP, SPAN, LANES), bf16),
        ] + [pltpu.SemaphoreType.DMA(count) for count in counts],
        compiler_params=pltpu.CompilerParams(
            collective_id=0, has_side_effects=True, vmem_limit_bytes=60 << 20
        ),
        cost_estimate=pl.CostEstimate(
            flops=20_000_000_000, bytes_accessed=12 << 20, transcendentals=0
        ),
        name="hyena_back",
    )(inputs, out_grad, out_weight, filt, *tables())
    return pl.pallas_call(
        hand_over,
        out_shape=tuple(jax.ShapeDtypeStruct(r.shape, r.dtype) for r in results),
        in_specs=[vmem] * 2,
        out_specs=(vmem, vmem),
        name="hand_over",
    )(*results)


def solution(mesh):
    in_specs = (P("seq", "chan"), P("seq", "chan"), P("chan", None), P("seq", "chan"))
    out_specs = (P("seq", "chan"), P("seq", "chan"))
    return jax.shard_map(
        per_device, mesh=mesh, in_specs=in_specs, out_specs=out_specs, check_vma=False
    )
```

time: 107 us -> 92.6 us (0.87)
  Pallas kernels: 102 us -> 91.3 us
  local copies, waits for them, and re-layouts: 3.93 us -> 0 us
    pallas_call x1, Pallas kernels: 102 us -> 89 us  [per_device(): pl.pallas_call(kernel, out_shape=(jax.ShapeDtypeStruct((SPAN, WIDTH), bf1...]
    unnamed x2 -> x0, local copies, waits for them, and re-layouts: 3.93 us -> none
    pallas_call x0 -> x1, Pallas kernels: none -> 2.38 us  [per_device(): pl.pallas_call(hand_over, out_shape=tuple((jax.ShapeDtypeStruct(r.shape,...]
where the time goes in v3:
time: 92.6 us; the launch traced here: 92 us
  Pallas kernels  91.3 us (99%)
    pallas_call x1, Pallas kernels, per_device(): pl.pallas_call(kernel, out_shape=(jax.ShapeDtypeStruct((SPAN, WIDTH), bf1...  89 us
    pallas_call x1, Pallas kernels, per_device(): pl.pallas_call(hand_over, out_shape=tuple((jax.ShapeDtypeStruct(r.shape,...  2.38 us

profile of v3, /device:TPU:1, one launch (start us, length us, event | category | flops | bytes accessed | tf_op | source)
XLA Modules:
  0.0 92.0 jit_solution(9871498337288558825)
XLA Ops:
  0.6 89.0 %hyena_back.1 = (bf16[1024,512]{1,0:T(8,128)(2,1)}, f32[128,512]{1,0:T(8,128)}) custom-call(bf16[1024,512]{1,0:T(8,128)(2,1)} %in_ref.1, bf16[1024,512]{1,0:T(8,128)(2,1)} %og_ref.1, bf16[512,4096]{1,0:T(8,128)(2,1)} %w_ref.1, f32[128,512]{1,0:T(8,128)} %filt_ref.1, bf16[512,512]{1,0:T(8,128)(2,1)} %constant.8.clone.fwd_hi, ...), custom_call_target="tpu_custom_call" | custom-call | flops 20000000000 | bytes 12582912 | tf_op jit(solution)/shard_map/hyena_back/pallas_call | solution.py:471
  89.6 2.4 %hand_over.1 = (bf16[1024,512]{1,0:T(8,128)(2,1)}, f32[128,512]{1,0:T(8,128)}) custom-call(bf16[1024,512]{1,0:T(8,128)(2,1)} %get-tuple-element.4.out_ref, f32[128,512]{1,0:T(8,128)} %get-tuple-element.5.fg_ref), custom_call_target="tpu_custom_call" | custom-call | tf_op jit(solution)/shard_map/hand_over/pallas_call | solution.py:507

commit v4 on v3

--- a/solution.py
+++ b/solution.py
@@ -39,11 +39,11 @@
 
 
 def tables():
-    freq = np.arange(HALF, dtype=np.int64)[:, None]
-    time = np.arange(FRAME, dtype=np.int64)[None, :]
+    freq = np.concatenate([np.arange(first, HALF, 2, dtype=np.int64) for first in range(2)])[:, None]
+    time = np.arange(BLOCK, dtype=np.int64)[None, :]
     angle = ((2 * freq + 1) * time % (2 * FRAME)).astype(np.float64) * (math.pi / FRAME)
     forward = np.concatenate([np.cos(angle), -np.sin(angle)], axis=0)
-    backward = forward[:, :BLOCK].T * (2.0 / FRAME)
+    backward = forward.T * (2.0 / FRAME)
     result = []
     for table in (forward, backward):
         result.extend(split_table(table.astype(np.float32)))
@@ -63,9 +63,9 @@
 
 
 def kernel(
-    in_ref, og_ref, w_ref, filt_ref, fwd_hi, fwd_lo, bwd_hi, bwd_lo,
+    in_ref, og_ref, w_ref, filt_ref, fwd_hi_ref, fwd_lo_ref, bwd_hi_ref, bwd_lo_ref,
     out_ref, fg_ref,
-    own, own_w,
+    own, own_w, fwd_hi, fwd_lo, bwd_hi, bwd_lo, spec,
     side, other_w, filt_all, values, part, got, grad, win, lag, val, acc, acc_lag,
     lag_out, lag_got, lag_sum, out_buf,
     x_send, x_recv, w_send, w_recv, f_send, f_recv, v_send, v_recv,
@@ -109,7 +109,15 @@
     values_own = pltpu.make_async_copy(
         in_ref.at[:, at(q * LANES, LANES)], values.at[at(q * SPAN, SPAN)], local_sem.at[3]
     )
+    table_loads = [
+        pltpu.make_async_copy(src, dst, local_sem.at[4 + n])
+        for n, (src, dst) in enumerate((
+            (fwd_hi_ref, fwd_hi), (fwd_lo_ref, fwd_lo), (bwd_hi_ref, bwd_hi), (bwd_lo_ref, bwd_lo)
+        ))
+    ]
     filter_own.start()
+    for load in table_loads:
+        load.start()
     own_load.start()
     weight_load.start()
     values_own.start()
@@ -226,8 +234,7 @@
         table[second] = wide[:, LANES:]
 
     def forward(wide):
-        width = wide.shape[0]
-        return dot(fwd_hi[:, :width], wide) + dot(fwd_lo[:, :width], wide)
+        return dot(fwd_hi[...], wide) + dot(fwd_lo[...], wide)
 
     def backward(wide):
         wide = wide.astype(jnp.bfloat16)
@@ -244,7 +251,7 @@
             )
             high = wide.astype(jnp.bfloat16)
             low = (wide - high.astype(jnp.float32)).astype(jnp.bfloat16)
-            put(lag, 2 * m, 2 * m + 1, forward(high) + dot(fwd_hi[:, :BLOCK], low))
+            put(lag, 2 * m, 2 * m + 1, forward(high) + dot(fwd_hi[...], low))
 
     def transform_values():
         values_own.wait()
@@ -257,14 +264,26 @@
                 [values[at((2 * n + e) * BLOCK, BLOCK), :] for e in range(2)], axis=1
             )))
 
-    def window(i):
-        return grad[pl.ds(pl.multiple_of(i * BLOCK, BLOCK), FRAME), :]
-
-    def transform_windows(first, pairs):
-        @pl.loop(0, pairs)
+    def transform_blocks(first):
+        def part_at(i):
+            return grad[at(i * BLOCK, BLOCK), :]
+
+        @pl.loop(0, (WINDOWS + 1) // PER_SPAN // 2)
         def _(j):
             i = first + 2 * PER_SPAN * j
-            put(win, i, i + PER_SPAN, forward(jnp.concatenate([window(i), window(i + PER_SPAN)], axis=1)))
+            put(spec, i, i + PER_SPAN, forward(
+                jnp.concatenate([part_at(i), part_at(i + PER_SPAN)], axis=1)
+            ))
+
+    def join(first):
+        @pl.loop(0, (WINDOWS - 1 - first) // PER_SPAN + 1)
+        def _(j):
+            i = first + PER_SPAN * j
+            for n in range(4):
+                rows = slice(n * HALF // 2, (n + 1) * HALF // 2)
+                cross = slice((n + 2) % 4 * HALF // 2, ((n + 2) % 4 + 1) * HALF // 2)
+                here, there = spec[i, rows, :], spec[i + 1, cross, :]
+                win[i, rows, :] = here + there if n in (0, 3) else here - there
 
     def multiply(side_of, t):
         rows = step_rows(t)
@@ -334,6 +353,23 @@
                             sums[n] = add(sums[n], f[i - n], w)
             for n in range(PER_SPAN):
                 acc[base + n, re, :], acc[base + n, im, :] = sums[n]
+
+    def sum_early(chosen, fresh):
+        spans = [i for i in range(WINDOWS) if i % PER_SPAN == chosen]
+
+        @pl.loop(0, HALF // ROWS)
+        def _(p):
+            re, im = bins(p)
+            f = [(lag[m, re, :], lag[m, im, :]) for m in range(LAGS)]
+            sums = {}
+            for i in spans:
+                w = (win[i, re, :], win[i, im, :])
+                for n in range(max(0, i - LAGS + 1), min(BLOCKS - 1, i) + 1):
+                    if n not in sums:
+                        sums[n] = None if fresh else (acc[n, re, :], acc[n, im, :])
+                    sums[n] = add(sums[n], f[i - n], w)
+                    if i + PER_SPAN > n + LAGS - 1 or i + PER_SPAN >= WINDOWS:
+                        acc[n, re, :], acc[n, im, :] = sums.pop(n)
 
     def sum_lags(classes, fresh):
         @pl.loop(0, HALF // ROWS)
@@ -370,6 +406,8 @@
         filter_to(k).wait_recv()
     start(*[filter_along(k) for k in (2, 1, 3)])
     pass_on(1)
+    for load in table_loads:
+        load.wait()
     transform_values()
     own_load.wait()
     weight_load.wait()
@@ -391,31 +429,31 @@
     pass_on(4)
     add_up(1)
     edge(0)
+    transform_blocks(0)
     edge(1)
+    transform_blocks(1)
     across(3)
     multiply(1, 3)
     multiply(0, 3)
     across(4)
     multiply(1, 4)
     multiply(0, 4)
-    transform_windows(0, 3)
-    for k in range(GROUP):
-        sum_inputs((q + k) % GROUP, (0,), True)
+    join(0)
+    sum_early(0, True)
     sum_lags((0,), True)
     add_up(2)
     edge(2)
-    transform_windows(1, 3)
+    transform_blocks(2)
+    join(1)
     add_up(3)
     add_up(4)
-    for k in range(GROUP):
-        sum_inputs((q + k) % GROUP, (1,), False)
+    sum_early(1, False)
     sum_lags((1,), False)
     edge(3)
     edge(4)
-    transform_windows(PER_SPAN - 2, 3)
-    transform_windows(PER_SPAN - 1, 2)
-    final = (WINDOWS - 1) - (WINDOWS - 1 - (PER_SPAN - 1)) % PER_SPAN
-    win[final] = forward(window(final))
+    transform_blocks(PER_SPAN - 1)
+    join(2)
+    join(3)
 
     def finish_span(k):
         place = (q + k) % GROUP
@@ -456,9 +494,24 @@
         lag_to(k).wait_recv()
 
 
-def hand_over(out_ref, fg_ref, out_final, fg_final):
-    out_final[...] = out_ref[...]
-    fg_final[...] = fg_ref[...]
+def hand_over(out_ref, fg_ref, out_final, fg_final, out_mid, fg_mid, sems):
+    parts = [(out_ref, out_mid, out_final, pl.ds(n * BLOCK, BLOCK)) for n in range(PER_SPAN)]
+    parts.append((fg_ref, fg_mid, fg_final, pl.ds(0, LAG_ROWS)))
+    arrive = [
+        pltpu.make_async_copy(a.at[rows], b.at[rows], sems.at[0, n])
+        for n, (a, b, _, rows) in enumerate(parts)
+    ]
+    leave = [
+        pltpu.make_async_copy(b.at[rows], c.at[rows], sems.at[1, n])
+        for n, (_, b, c, rows) in enumerate(parts)
+    ]
+    for copy in arrive:
+        copy.start()
+    for first, second in zip(arrive, leave):
+        first.wait()
+        second.start()
+    for copy in leave:
+        copy.wait()
 
 
 def per_device(inputs, out_grad, out_weight, filt):
@@ -467,18 +520,23 @@
     bf16, f32 = jnp.bfloat16, jnp.float32
     steps = len(STEPS)
     counts = [(4, steps)] * 2 + [(2 * RING,)] * 2 + [(2, GROUP)] * 2 + [(GROUP,)] * 2
-    counts += [(2, GROUP, steps)] * 2 + [(2, steps)] * 2 + [(GROUP,)] * 2 + [(2, GROUP)] * 2 + [(4,)]
+    counts += [(2, GROUP, steps)] * 2 + [(2, steps)] * 2 + [(GROUP,)] * 2 + [(2, GROUP)] * 2 + [(8,)]
     results = pl.pallas_call(
         kernel,
         out_shape=(
             jax.ShapeDtypeStruct((SPAN, WIDTH), bf16),
             jax.ShapeDtypeStruct((LAG_ROWS, WIDTH), f32),
         ),
-        in_specs=[anywhere] * 4 + [vmem] * 4,
+        in_specs=[anywhere] * 8,
         out_specs=(vmem, vmem),
         scratch_shapes=[
             pltpu.VMEM((SPAN, WIDTH), bf16),
             pltpu.VMEM((WIDTH, SHARE), bf16),
+            pltpu.VMEM((FRAME, BLOCK), bf16),
+            pltpu.VMEM((FRAME, BLOCK), bf16),
+            pltpu.VMEM((BLOCK, FRAME), bf16),
+            pltpu.VMEM((BLOCK, FRAME), bf16),
+            pltpu.VMEM((WINDOWS + 1, FRAME, LANES), f32),
             pltpu.VMEM((3, SPAN, WIDTH), bf16),
             pltpu.VMEM((WIDTH, SHARE), bf16),
             pltpu.VMEM((LAG_LEN, LANES), f32),
@@ -507,8 +565,13 @@
     return pl.pallas_call(
         hand_over,
         out_shape=tuple(jax.ShapeDtypeStruct(r.shape, r.dtype) for r in results),
-        in_specs=[vmem] * 2,
-        out_specs=(vmem, vmem),
+        in_specs=[anywhere] * 2,
+        out_specs=(anywhere, anywhere),
+        scratch_shapes=[
+            pltpu.VMEM((SPAN, WIDTH), bf16),
+            pltpu.VMEM((LAG_ROWS, WIDTH), f32),
+            pltpu.SemaphoreType.DMA((2, PER_SPAN + 1)),
+        ],
         name="hand_over",
     )(*results)
 

time: 92.6 us -> 86.6 us (0.935)
  Pallas kernels: 91.3 us -> 85.9 us
    pallas_call x1, Pallas kernels: 89 us -> 83.8 us  [per_device(): pl.pallas_call(kernel, out_shape=(jax.ShapeDtypeStruct((SPAN, WIDTH), bf1...]
where the time goes in v4:
time: 86.6 us; the launch traced here: 86.5 us
  Pallas kernels  85.9 us (99%)
    pallas_call x1, Pallas kernels, per_device(): pl.pallas_call(kernel, out_shape=(jax.ShapeDtypeStruct((SPAN, WIDTH), bf1...  83.8 us
    pallas_call x1, Pallas kernels, per_device(): pl.pallas_call(hand_over, out_shape=tuple((jax.ShapeDtypeStruct(r.shape,...  2.08 us

profile of v4, /device:TPU:1, one launch (start us, length us, event | category | flops | bytes accessed | tf_op | source)
XLA Modules:
  0.0 86.5 jit_solution(9437881064512894571)
XLA Ops:
  0.6 83.8 %hyena_back.1 = (bf16[1024,512]{1,0:T(8,128)(2,1)}, f32[128,512]{1,0:T(8,128)}) custom-call(bf16[1024,512]{1,0:T(8,128)(2,1)} %in_ref.1, bf16[1024,512]{1,0:T(8,128)(2,1)} %og_ref.1, bf16[512,4096]{1,0:T(8,128)(2,1)} %w_ref.1, f32[128,512]{1,0:T(8,128)} %filt_ref.1, bf16[512,256]{1,0:T(8,128)(2,1)} %constant.8.clone.fwd_hi_ref, ...), custom_call_target="tpu_custom_call" | custom-call | flops 20000000000 | bytes 12582912 | tf_op jit(solution)/shard_map/hyena_back/pallas_call | solution.py:524
  84.4 2.1 %hand_over.1 = (bf16[1024,512]{1,0:T(8,128)(2,1)}, f32[128,512]{1,0:T(8,128)}) custom-call(bf16[1024,512]{1,0:T(8,128)(2,1)} %get-tuple-element.4.out_ref, f32[128,512]{1,0:T(8,128)} %get-tuple-element.5.fg_ref), custom_call_target="tpu_custom_call" | custom-call | tf_op jit(solution)/shard_map/hand_over/pallas_call | solution.py:565

commit v5 on v4

--- a/solution.py
+++ b/solution.py
@@ -18,7 +18,7 @@
 GROUP = 4
 RING = 4
 SPAN = 1024
-STEPS = ((0, 256), (256, 256), (512, 256), (768, 128), (896, 128))
+STEPS = ((0, 256), (256, 256), (512, 256), (768, 160), (928, 96))
 PER_SPAN = SPAN // BLOCK
 AHEAD = 2
 WIDTH = 512
@@ -315,7 +315,7 @@
                 near = part[0, owner, rows]
             total = near.astype(jnp.float32) + got[1, owner, rows].astype(jnp.float32)
             begin, size = STEPS[t]
-            grad[pl.ds(pl.multiple_of(owner * SPAN + begin, LANES), size), :] = total.astype(jnp.bfloat16)
+            grad[pl.ds(pl.multiple_of(owner * SPAN + begin, 2 * ROWS), size), :] = total.astype(jnp.bfloat16)
         for i in range(2):
             start(halo(i, t))
 
@@ -430,23 +430,23 @@
     add_up(1)
     edge(0)
     transform_blocks(0)
-    edge(1)
-    transform_blocks(1)
     across(3)
     multiply(1, 3)
     multiply(0, 3)
     across(4)
     multiply(1, 4)
     multiply(0, 4)
+    edge(1)
+    transform_blocks(1)
     join(0)
+    add_up(2)
     sum_early(0, True)
     sum_lags((0,), True)
-    add_up(2)
+    add_up(3)
+    add_up(4)
     edge(2)
     transform_blocks(2)
     join(1)
-    add_up(3)
-    add_up(4)
     sum_early(1, False)
     sum_lags((1,), False)
     edge(3)
@@ -467,7 +467,6 @@
             start(out_to(k))
 
     finish_span(2)
-    finish_span(3)
     sum_lags((2, 3), False)
     for k in (2, 1, 3, 0):
         place = (z + k) % RING
@@ -476,6 +475,7 @@
             lag_out[at((2 * place + e) * BLOCK, BLOCK), :] = wide[:, e * LANES:(e + 1) * LANES]
         if k:
             start(lag_along(k))
+    finish_span(3)
     finish_span(1)
     finish_span(0)
     out_ref[:, at(q * LANES, LANES)] = out_buf[q]

time: 86.6 us -> 82.8 us (0.956)
  Pallas kernels: 85.9 us -> 82.1 us
    pallas_call x1, Pallas kernels: 83.8 us -> 80 us  [per_device(): pl.pallas_call(kernel, out_shape=(jax.ShapeDtypeStruct((SPAN, WIDTH), bf1...]
where the time goes in v5:
time: 82.8 us; the launch traced here: 82.7 us
  Pallas kernels  82.1 us (99%)
    pallas_call x1, Pallas kernels, per_device(): pl.pallas_call(kernel, out_shape=(jax.ShapeDtypeStruct((SPAN, WIDTH), bf1...  80 us
    pallas_call x1, Pallas kernels, per_device(): pl.pallas_call(hand_over, out_shape=tuple((jax.ShapeDtypeStruct(r.shape,...  2.08 us

profile of v5, /device:TPU:1, one launch (start us, length us, event | category | flops | bytes accessed | tf_op | source)
XLA Modules:
  0.0 82.7 jit_solution(14254553089188783530)
XLA Ops:
  0.6 80.0 %hyena_back.1 = (bf16[1024,512]{1,0:T(8,128)(2,1)}, f32[128,512]{1,0:T(8,128)}) custom-call(bf16[1024,512]{1,0:T(8,128)(2,1)} %in_ref.1, bf16[1024,512]{1,0:T(8,128)(2,1)} %og_ref.1, bf16[512,4096]{1,0:T(8,128)(2,1)} %w_ref.1, f32[128,512]{1,0:T(8,128)} %filt_ref.1, bf16[512,256]{1,0:T(8,128)(2,1)} %constant.8.clone.fwd_hi_ref, ...), custom_call_target="tpu_custom_call" | custom-call | flops 20000000000 | bytes 12582912 | tf_op jit(solution)/shard_map/hyena_back/pallas_call | solution.py:524
  80.6 2.1 %hand_over.1 = (bf16[1024,512]{1,0:T(8,128)(2,1)}, f32[128,512]{1,0:T(8,128)}) custom-call(bf16[1024,512]{1,0:T(8,128)(2,1)} %get-tuple-element.4.out_ref, f32[128,512]{1,0:T(8,128)} %get-tuple-element.5.fg_ref), custom_call_target="tpu_custom_call" | custom-call | tf_op jit(solution)/shard_map/hand_over/pallas_call | solution.py:565

commit v6 on v5

--- a/solution.py
+++ b/solution.py
@@ -329,10 +329,24 @@
                 begin, size = STEPS[t]
                 grad[pl.ds((GROUP + i) * SPAN + begin, size), :] = jnp.zeros((size, LANES), jnp.bfloat16)
 
+    def triple(pair):
+        return pair[0], pair[1], pair[0] - pair[1]
+
+    def spread(pair):
+        return pair[0], pair[1] - pair[0], pair[0] + pair[1]
+
     def add(total, k, w):
-        r = k[0] * w[0] + k[1] * w[1]
-        i = k[0] * w[1] - k[1] * w[0]
-        return (r, i) if total is None else (total[0] + r, total[1] + i)
+        terms = (k[2] * w[0], k[0] * w[1], k[1] * w[2])
+        return terms if total is None else tuple(a + b for a, b in zip(total, terms))
+
+    def settle(total):
+        return total[0] + total[2], total[0] + total[1]
+
+    def store(table, n, re, im, total, fresh):
+        total = settle(total)
+        if not fresh:
+            total = (total[0] + table[n, re, :], total[1] + table[n, im, :])
+        table[n, re, :], table[n, im, :] = total
 
     def bins(p):
         return at(p * ROWS, ROWS), at(HALF + p * ROWS, ROWS)
@@ -343,16 +357,16 @@
         @pl.loop(0, HALF // ROWS)
         def _(p):
             re, im = bins(p)
-            f = [(lag[m, re, :], lag[m, im, :]) for m in range(LAGS)]
-            sums = [None if fresh else (acc[base + n, re, :], acc[base + n, im, :]) for n in range(PER_SPAN)]
+            f = [triple((lag[m, re, :], lag[m, im, :])) for m in range(LAGS)]
+            sums = [None] * PER_SPAN
             for i in range(PER_SPAN + LAGS - 1):
                 if i % PER_SPAN in classes:
-                    w = (win[base + i, re, :], win[base + i, im, :])
+                    w = spread((win[base + i, re, :], win[base + i, im, :]))
                     for n in range(PER_SPAN):
                         if 0 <= i - n < LAGS:
                             sums[n] = add(sums[n], f[i - n], w)
             for n in range(PER_SPAN):
-                acc[base + n, re, :], acc[base + n, im, :] = sums[n]
+                store(acc, base + n, re, im, sums[n], fresh)
 
     def sum_early(chosen, fresh):
         spans = [i for i in range(WINDOWS) if i % PER_SPAN == chosen]
@@ -360,31 +374,29 @@
         @pl.loop(0, HALF // ROWS)
         def _(p):
             re, im = bins(p)
-            f = [(lag[m, re, :], lag[m, im, :]) for m in range(LAGS)]
+            f = [triple((lag[m, re, :], lag[m, im, :])) for m in range(LAGS)]
             sums = {}
             for i in spans:
-                w = (win[i, re, :], win[i, im, :])
+                w = spread((win[i, re, :], win[i, im, :]))
                 for n in range(max(0, i - LAGS + 1), min(BLOCKS - 1, i) + 1):
-                    if n not in sums:
-                        sums[n] = None if fresh else (acc[n, re, :], acc[n, im, :])
-                    sums[n] = add(sums[n], f[i - n], w)
+                    sums[n] = add(sums.get(n), f[i - n], w)
                     if i + PER_SPAN > n + LAGS - 1 or i + PER_SPAN >= WINDOWS:
-                        acc[n, re, :], acc[n, im, :] = sums.pop(n)
+                        store(acc, n, re, im, sums.pop(n), fresh)
 
     def sum_lags(classes, fresh):
         @pl.loop(0, HALF // ROWS)
         def _(p):
             re, im = bins(p)
-            sums = [None if fresh else (acc_lag[m, re, :], acc_lag[m, im, :]) for m in range(LAGS)]
+            sums = [None] * LAGS
             for i in range(WINDOWS):
                 if i % PER_SPAN in classes:
-                    w = (win[i, re, :], win[i, im, :])
+                    w = spread((win[i, re, :], win[i, im, :]))
                     for m in range(LAGS):
                         n = i - m
                         if 0 <= n < BLOCKS:
-                            sums[m] = add(sums[m], (val[n, re, :], val[n, im, :]), w)
+                            sums[m] = add(sums[m], triple((val[n, re, :], val[n, im, :])), w)
             for m in range(LAGS):
-                acc_lag[m, re, :], acc_lag[m, im, :] = sums[m]
+                store(acc_lag, m, re, im, sums[m], fresh)
 
     start(*direct(0))
     start(weight(0), weight(2))
@@ -422,11 +434,11 @@
     multiply(0, 1)
     add_up(0)
     pass_on(3)
-    transform_filter()
     across(2)
     multiply(1, 2)
     multiply(0, 2)
     pass_on(4)
+    transform_filter()
     add_up(1)
     edge(0)
     transform_blocks(0)
@@ -466,6 +478,7 @@
         if k:
             start(out_to(k))
 
+    settled = len(sends)
     finish_span(2)
     sum_lags((2, 3), False)
     for k in (2, 1, 3, 0):
@@ -479,6 +492,8 @@
     finish_span(1)
     finish_span(0)
     out_ref[:, at(q * LANES, LANES)] = out_buf[q]
+    for copy in sends[:settled]:
+        copy.wait_send()
     total = lag_out[at(z * LAG_SHARE, LAG_SHARE), :].astype(jnp.float32)
     for k in range(1, RING):
         lag_along(k).wait_recv()
@@ -487,7 +502,7 @@
     for k in (2, 3, 1):
         start(lag_to(k))
     fg_ref[:, at(q * LANES, LANES)] = lag_sum[at(q * LAG_ROWS, LAG_ROWS), :]
-    for copy in sends:
+    for copy in sends[settled:]:
         copy.wait_send()
     for k in range(1, GROUP):
         out_to(k).wait_recv()

time: 82.8 us -> 82.1 us (level)
  no operation moved by 1% of the time
where the time goes in v6:
time: 82.1 us; the launch traced here: 81.9 us
  Pallas kernels  81.3 us (99%)
    pallas_call x1, Pallas kernels, per_device(): pl.pallas_call(kernel, out_shape=(jax.ShapeDtypeStruct((SPAN, WIDTH), bf1...  79.2 us
    pallas_call x1, Pallas kernels, per_device(): pl.pallas_call(hand_over, out_shape=tuple((jax.ShapeDtypeStruct(r.shape,...  2.08 us

profile of v6, /device:TPU:1, one launch (start us, length us, event | category | flops | bytes accessed | tf_op | source)
XLA Modules:
  0.0 81.9 jit_solution(7899051629121932011)
XLA Ops:
  0.6 79.2 %hyena_back.1 = (bf16[1024,512]{1,0:T(8,128)(2,1)}, f32[128,512]{1,0:T(8,128)}) custom-call(bf16[1024,512]{1,0:T(8,128)(2,1)} %in_ref.1, bf16[1024,512]{1,0:T(8,128)(2,1)} %og_ref.1, bf16[512,4096]{1,0:T(8,128)(2,1)} %w_ref.1, f32[128,512]{1,0:T(8,128)} %filt_ref.1, bf16[512,256]{1,0:T(8,128)(2,1)} %constant.8.clone.fwd_hi_ref, ...), custom_call_target="tpu_custom_call" | custom-call | flops 20000000000 | bytes 12582912 | tf_op jit(solution)/shard_map/hyena_back/pallas_call | solution.py:539
  79.8 2.1 %hand_over.1 = (bf16[1024,512]{1,0:T(8,128)(2,1)}, f32[128,512]{1,0:T(8,128)}) custom-call(bf16[1024,512]{1,0:T(8,128)(2,1)} %get-tuple-element.4.out_ref, f32[128,512]{1,0:T(8,128)} %get-tuple-element.5.fg_ref), custom_call_target="tpu_custom_call" | custom-call | tf_op jit(solution)/shard_map/hand_over/pallas_call | solution.py:580
